TPU v7x, 768 devices: a whole 4x8x12 slice. The times are simulated.
768 devices in a mesh: rep: 12 (over z), bal: 8 (over y), tab: 8 (over x, core).
Axes of the slice: x: 4, y: 8, z: 12, core: 2. Of those that a mesh axis runs over, the one named last changes fastest.
Arguments:
- hot_rows: float32 [245760, 1024], P(('rep', 'bal', 'tab')), may hold values from -640 to 640
- cold_rows: bfloat16 [245760, 1024], P(('rep', 'bal', 'tab')), may hold values from -640 to 640
- row_source: int32 [294912, 1], P(('rep', 'bal', 'tab')), may hold values from 0 to 15; in each aligned block of 384 rows (0 to 383, 384 to 767, ...) at most 40 rows name the same one
- lengths: int32 [12, 8, 8, 8], P('rep', None, 'tab'), may hold values from 8 to 88, as said below
- destination: int32 [12, 8, 8, 8], P('rep', None, 'tab'), may hold values from 0 to 7, as said below
- proj_weight: bfloat16 [1024, 4096], replicated, may hold values from -0.1875 to 0.1875
- out_grad: bfloat16 [294912, 1024], P(('rep', 'bal', 'tab')), may hold values from -0.01171875 to 0.01171875
Outputs:
- attention_out: bfloat16 [294912, 1024], P(('rep', 'bal', 'tab'))
- grad_out_proj: bfloat16 [1024, 1024], P(('bal', 'tab'))
Inputs may be any that keep to these rules, and one draw needn't show every extreme that they name: `row_source`: code shard + 8 * tier of each position's row (tier 0 float32, tier 1 bfloat16); among the positions of one device no code occurs more than 40 times. lengths[r, s, t, h] is the length of history h of device (r, s, t); each device's lengths sum to 384; the histories that the devices of one bal group send to any one of them also sum to 384; the devices of one bal group hold the same lengths in different orders, and each group has a history of exactly 88. destination[r, s, t, :] is a permutation of 0 to 7: every device sends one history to each device of its bal group.
All inputs are finite; a program needn't handle non-finite values.
Results may differ from a plain program's by a relative error of at most 0.02.
Values may be sent and summed in bfloat16 or wider, within the bound.
A program may use at most 64 MiB of HBM per device.

v0:
```python
import jax
import jax.numpy as jnp
from jax import lax
from jax.sharding import PartitionSpec as P

HEADS = 8


def layer_norm(rows_in):
    center = jnp.mean(rows_in, axis=-1, keepdims=True)
    centered = rows_in - center
    deviation = jnp.mean(centered * centered, axis=-1, keepdims=True)
    return centered * lax.rsqrt(deviation + 1e-05)


def on_device(hot_rows, cold_rows, row_source, lengths, destination, proj_weight, out_grad):
    tab_count = lax.axis_size("tab")
    bal_count = lax.axis_size("bal")
    home_rows = row_source.shape[0]
    model_width = proj_weight.shape[0]
    slot_count = hot_rows.shape[0] // tab_count
    code_count = 2 * tab_count
    row_codes = row_source[:, 0]
    code_ids = jnp.arange(code_count, dtype=jnp.int32)
    code_flags = (row_codes[:, None] == code_ids[None, :]).astype(jnp.int32)
    earlier = jnp.cumsum(code_flags, axis=0, dtype=jnp.int32) - code_flags
    slot_index = jnp.sum(earlier * code_flags, axis=1, dtype=jnp.int32)
    buffer_index = row_codes * slot_count + slot_index
    hot_parts = hot_rows.reshape(tab_count, slot_count, model_width)
    cold_parts = cold_rows.reshape(tab_count, slot_count, model_width)
    hot_in = lax.all_to_all(hot_parts, "tab", split_axis=0, concat_axis=0, tiled=True)
    cold_in = lax.all_to_all(cold_parts, "tab", split_axis=0, concat_axis=0, tiled=True)
    tier_rows = tab_count * slot_count
    tier_ids = row_codes // tab_count
    local_index = jnp.where(tier_ids == 0, buffer_index, buffer_index - tier_rows)
    hot_pick = jnp.take(hot_in.reshape(tier_rows, model_width), local_index, axis=0)
    cold_pick = jnp.take(cold_in.reshape(tier_rows, model_width), local_index, axis=0).astype(
        jnp.float32
    )
    picked = jnp.where(tier_ids[:, None] == 0, hot_pick, cold_pick)
    normed = layer_norm(picked).astype(jnp.bfloat16)
    mean_len = home_rows // bal_count
    capacity = 2 * mean_len - mean_len // 6
    own_index = lax.axis_index("bal")
    group_len = lengths.reshape(bal_count, bal_count)
    group_dest = destination.reshape(bal_count, bal_count)
    own_len = group_len[own_index]
    own_dest = group_dest[own_index]
    own_start = jnp.cumsum(own_len, dtype=jnp.int32) - own_len
    peer_ids = jnp.arange(bal_count, dtype=jnp.int32)
    chosen = (own_dest[None, :] == peer_ids[:, None]).astype(jnp.int32)
    send_len = jnp.sum(chosen * own_len[None, :], axis=1, dtype=jnp.int32)
    send_start = jnp.sum(chosen * own_start[None, :], axis=1, dtype=jnp.int32)
    offsets = jnp.arange(capacity, dtype=jnp.int32)
    source_rows = jnp.minimum(send_start[:, None] + offsets[None, :], home_rows - 1)
    live_slot = offsets[None, :] < send_len[:, None]
    gathered = jnp.take(normed, source_rows.reshape(-1), axis=0).reshape(
        bal_count, capacity, model_width
    )
    outgoing = jnp.where(live_slot[:, :, None], gathered, jnp.zeros((), jnp.bfloat16))
    incoming = lax.all_to_all(outgoing, "bal", split_axis=0, concat_axis=0, tiled=True)
    arriving = (group_dest == own_index).astype(jnp.int32)
    in_len = jnp.sum(arriving * group_len, axis=1, dtype=jnp.int32)
    in_end = jnp.cumsum(in_len, dtype=jnp.int32)
    in_off = in_end - in_len
    positions = jnp.arange(home_rows, dtype=jnp.int32)
    segment = jnp.sum(
        (in_end[None, :] <= positions[:, None]).astype(jnp.int32), axis=1, dtype=jnp.int32
    )
    segment_flags = (segment[:, None] == peer_ids[None, :]).astype(jnp.int32)
    segment_off = jnp.sum(segment_flags * in_off[None, :], axis=1, dtype=jnp.int32)
    balanced = jnp.take(
        incoming.reshape(bal_count * capacity, model_width),
        segment * capacity + positions - segment_off,
        axis=0,
    )
    head_count = HEADS
    head_size = model_width // head_count
    projected = jax.nn.silu(
        jnp.dot(balanced, proj_weight, preferred_element_type=jnp.float32)
    ).astype(jnp.bfloat16)
    gating = projected[:, :model_width]
    values = projected[:, model_width : 2 * model_width].reshape(home_rows, head_count, head_size)
    queries = projected[:, 2 * model_width : 3 * model_width].reshape(
        home_rows, head_count, head_size
    )
    key_rows = projected[:, 3 * model_width :].reshape(home_rows, head_count, head_size)
    scores = jnp.einsum(
        "ihd,jhd->hij", queries, key_rows, preferred_element_type=jnp.float32
    ) * head_size ** (-0.5)
    allowed = (segment[:, None] == segment[None, :]) & (positions[None, :] <= positions[:, None])
    weights = jnp.where(allowed[None], jax.nn.silu(scores), 0.0).astype(jnp.bfloat16)
    attention_sum = jnp.einsum(
        "hij,jhd->ihd", weights, values, preferred_element_type=jnp.float32
    ).reshape(home_rows, model_width)
    attended = (layer_norm(attention_sum) * gating.astype(jnp.float32)).astype(jnp.bfloat16)
    shared = lax.psum_scatter(
        lax.dot_general(
            out_grad, attended, (((0,), (0,)), ((), ())), preferred_element_type=jnp.float32
        ),
        ("bal", "tab"),
        scatter_dimension=0,
        tiled=True,
    )
    total = lax.psum(shared.astype(jnp.bfloat16), "rep")
    return (attended, total)


def solution(mesh):
    in_specs = (
        P(("rep", "bal", "tab"), None),
        P(("rep", "bal", "tab"), None),
        P(("rep", "bal", "tab"), None),
        P("rep", None, "tab", None),
        P("rep", None, "tab", None),
        P(),
        P(("rep", "bal", "tab"), None),
    )
    out_specs = (P(("rep", "bal", "tab"), None), P(("bal", "tab"), None))
    return jax.shard_map(
        on_device, mesh=mesh, in_specs=in_specs, out_specs=out_specs, check_vma=False
    )
```

profile of v0, /device:TPU:16, one launch (start us, length us, event | category | flops | bytes accessed | tf_op | source)
XLA Modules:
  0.0 347.3 jit_solution(14484326303792313029)
XLA Ops:
  7.2 4.4 %all-to-all-start.1 = ((bf16[8,40,1024]{2,1,0:T(8,128)(2,1)}), bf16[8,40,1024]{2,1,0:T(8,128)(2,1)S(1)}, u32[]{:S(2)}, u32[]{:S(2)}) async-start(bf16[8,40,1024]{2,1,0:T(8,128)(2,1)} %bitcast.78), calls=%async_computation.1 | async-start | bytes 1310720 | tf_op jit(solution)/shard_map/all_to_all | solution.py:32
  13.9 0.8 reduce-window.27
  15.6 7.7 %all-to-all-done.1 = bf16[8,40,1024]{2,1,0:T(8,128)(2,1)S(1)} async-done(((bf16[8,40,1024]{2,1,0:T(8,128)(2,1)}), bf16[8,40,1024]{2,1,0:T(8,128)(2,1)S(1)}, u32[]{:S(2)}, u32[]{:S(2)}) %all-to-all-start.1) | async-done | bytes 655392 | tf_op jit(solution)/shard_map/all_to_all | solution.py:32
  23.4 3.6 %all-to-all-start = ((f32[8,40,1024]{2,1,0:T(8,128)}), f32[8,40,1024]{2,1,0:T(8,128)S(1)}, u32[]{:S(2)}, u32[]{:S(2)}) async-start(f32[8,40,1024]{2,1,0:T(8,128)} %bitcast.76), calls=%async_computation | async-start | bytes 2621440 | tf_op jit(solution)/shard_map/all_to_all | solution.py:31
  28.2 2.1 gather_fusion.1
  30.2 15.4 %all-to-all-done = f32[8,40,1024]{2,1,0:T(8,128)S(1)} async-done(((f32[8,40,1024]{2,1,0:T(8,128)}), f32[8,40,1024]{2,1,0:T(8,128)S(1)}, u32[]{:S(2)}, u32[]{:S(2)}) %all-to-all-start) | async-done | bytes 1310752 | tf_op jit(solution)/shard_map/all_to_all | solution.py:31
  45.6 2.5 gather_fusion
  48.1 2.0 fusion.33
  51.2 3.5 %gather_fusion.2 = bf16[704,1024]{1,0:T(8,128)(2,1)} fusion(bf16[384,1024]{1,0:T(8,128)(2,1)S(1)} %multiply_convert_fusion.2, s32[1024]{0:T(1024)S(1)} %pad_clamp_fusion.1), kind=kCustom, calls=%fused_computation.2 | custom fusion | bytes 2886400 | tf_op jit(solution)/shard_map/jit(_take)/gather | solution.py:57
  54.7 2.7 select_select_fusion
  57.5 12.1 %all-to-all-start.2 = ((bf16[8,88,1024]{2,1,0:T(8,128)(2,1)}), bf16[8,88,1024]{2,1,0:T(8,128)(2,1)S(1)}, u32[]{:S(2)}, u32[]{:S(2)}) async-start(bf16[8,88,1024]{2,1,0:T(8,128)(2,1)} %select_select_fusion), calls=%async_computation.2 | async-start | bytes 2883584 | tf_op jit(solution)/shard_map/all_to_all | solution.py:61
  70.4 34.1 %all-to-all-done.2 = bf16[8,88,1024]{2,1,0:T(8,128)(2,1)S(1)} async-done(((bf16[8,88,1024]{2,1,0:T(8,128)(2,1)}), bf16[8,88,1024]{2,1,0:T(8,128)(2,1)S(1)}, u32[]{:S(2)}, u32[]{:S(2)}) %all-to-all-start.2) | async-done | bytes 1441824 | tf_op jit(solution)/shard_map/all_to_all | solution.py:61
  104.5 2.7 gather_fusion.3
  107.2 7.5 %multiply_convert_fusion = bf16[384,4096]{1,0:T(8,128)(2,1)S(1)} fusion(bf16[1024,4096]{1,0:T(8,128)(2,1)} %param.12, bf16[384,1024]{1,0:T(8,128)(2,1)} %gather_fusion.3, pred[384]{0:T(512)(128)(4,1)S(1)} %compare_and_fusion.1), kind=kOutput, calls=%fused_computation.4 | convolution fusion | flops 3229483008 | bytes 12321152 | tf_op jit(solution)/shard_map/dot_general | solution.py:80
  114.8 1.7 slice_bitcast_fusion.1
  116.9 1.2 copy.32
  118.0 3.8 %fusion.35 = (f32[384]{0:T(512)S(1)}, f32[8,128,384]{2,1,0:T(8,128)S(1)}) fusion(bf16[384,8,128]{0,2,1:T(8,128)(2,1)} %bitcast.77, pred[384,384]{1,0:T(8,128)(4,1)S(1)} %fusion.18, bf16[48,8,8,128]{3,2,1,0:T(8,128)(2,1)} %get-tuple-element.19, bf16[48,8,8,128]{3,2,1,0:T(8,128)(2,1)} %get-tuple-element.18), kind=kOutput, calls=%fused_computation.84 | convolution fusion | flops 612630144 | bytes 4081152 | tf_op jit(solution)/shard_map/hij,jhd->ihd/dot_general | solution.py:93
  122.1 1.6 copy.33
  123.7 1.9 multiply_convert_fusion.1
  125.6 3.3 convolution_bitcast_fusion
  128.9 5.3 %copy.34 = f32[1024,1024]{1,0:T(8,128)} copy(f32[1024,1024]{0,1:T(8,128)} %convolution_bitcast_fusion) | data formatting | bytes 8388608
  134.3 156.7 %reduce-scatter.4.cloned.1.call-done = f32[16,1024]{1,0:T(8,128)} async-done(((f32[1024,1024]{1,0:T(8,128)}), f32[16,1024]{1,0:T(8,128)}) %reduce-scatter.4.cloned.1.call-update) | async-done | bytes 65552
  291.0 1.0 copy.35
  292.0 47.7 %psum.7 = bf16[16,1024]{0,1:T(8,128)(2,1)S(1)} all-reduce(bf16[16,1024]{0,1:T(8,128)(2,1)S(1)} %copy.35), channel_id=1, replica_groups=mesh['rep'=12,'bal'=8,'tab'=8] {'rep'}, use_global_device_ids=true, to_apply=%region_15.16 | all-reduce | flops 16384 | bytes 65536 | tf_op jit(solution)/shard_map/psum | solution.py:105
  (57 shorter events, 7.6 us)
Async XLA Ops:
  7.2 118.5 %copy-start = (bf16[384,1024]{1,0:T(8,128)(2,1)S(1)}, bf16[384,1024]{1,0:T(8,128)(2,1)}, u32[]{:S(2)}) copy-start(bf16[384,1024]{1,0:T(8,128)(2,1)} %param.13) | copy-start | bytes 2359300
  7.2 16.2 %all-to-all-start.1 = ((bf16[8,40,1024]{2,1,0:T(8,128)(2,1)}), bf16[8,40,1024]{2,1,0:T(8,128)(2,1)S(1)}, u32[]{:S(2)}, u32[]{:S(2)}) async-start(bf16[8,40,1024]{2,1,0:T(8,128)(2,1)} %bitcast.78), calls=%async_computation.1 | async-start | bytes 1310720 | tf_op jit(solution)/shard_map/all_to_all | solution.py:32
  11.6 15.8 %copy-start.4 = (s32[384,1]{0,1:T(1,128)S(1)}, s32[384,1]{0,1:T(1,128)}, u32[]{:S(2)}) copy-start(s32[384,1]{0,1:T(1,128)} %param.9) | copy-start | bytes 4612
  23.4 22.3 %all-to-all-start = ((f32[8,40,1024]{2,1,0:T(8,128)}), f32[8,40,1024]{2,1,0:T(8,128)S(1)}, u32[]{:S(2)}, u32[]{:S(2)}) async-start(f32[8,40,1024]{2,1,0:T(8,128)} %bitcast.76), calls=%async_computation | async-start | bytes 2621440 | tf_op jit(solution)/shard_map/all_to_all | solution.py:31
  48.1 2.0 copy-start.1
  51.2 3.5 %copy-start.6 = (pred[8,88]{1,0:T(8,128)(4,1)S(1)}, pred[8,88]{1,0:T(8,128)(4,1)}, u32[]{:S(2)}) copy-start(pred[8,88]{1,0:T(8,128)(4,1)} %get-tuple-element.23) | copy-start | bytes 2116
  51.2 3.5 %copy-start.7 = (pred[8,88]{1,0:T(8,128)(4,1)S(1)}, pred[8,88]{1,0:T(8,128)(4,1)}, u32[]{:S(2)}) copy-start(pred[8,88]{1,0:T(8,128)(4,1)} %get-tuple-element.24) | copy-start | bytes 2116
  57.5 12.1 %copy-start.5 = (s32[1,8,1,8]{3,2,1,0:T(1,128)S(1)}, s32[1,8,1,8]{3,2,1,0:T(1,128)}, u32[]{:S(2)}) copy-start(s32[1,8,1,8]{3,2,1,0:T(1,128)} %param.10) | copy-start | bytes 772
  57.5 12.1 %copy-start.8 = (s32[1,8,1,8]{3,2,1,0:T(1,128)S(1)}, s32[1,8,1,8]{3,2,1,0:T(1,128)}, u32[]{:S(2)}) copy-start(s32[1,8,1,8]{3,2,1,0:T(1,128)} %param.11) | copy-start | bytes 772
  57.5 47.0 %all-to-all-start.2 = ((bf16[8,88,1024]{2,1,0:T(8,128)(2,1)}), bf16[8,88,1024]{2,1,0:T(8,128)(2,1)S(1)}, u32[]{:S(2)}, u32[]{:S(2)}) async-start(bf16[8,88,1024]{2,1,0:T(8,128)(2,1)} %select_select_fusion), calls=%async_computation.2 | async-start | bytes 2883584 | tf_op jit(solution)/shard_map/all_to_all | solution.py:61
  69.6 221.4 %reduce-scatter.4.cloned.1.call-start = ((), (), s32[]{:S(2)}) async-start(), calls=%async_computation.4 | async-start | bytes 4259840
  114.8 2.1 copy-start.3
  125.6 3.3 copy-start.2
Sparse Core Ops, SparseCore 0:
  134.4 156.5 reduce-scatter.3
where the time goes:
time: 348 us; the launch traced here: 347 us
  waiting for transfers between devices  214 us (61%)
  blocking collectives  47.7 us (14%)
  local copies, waits for them, and re-layouts  24.3 us (7%)
  starting transfers between devices  20.1 us (6%)
  matrix products  14.6 us (4%)
  between operations  14.2 us (4%)
  other arithmetic  12.3 us (4%)
    unnamed x2, waiting for transfers between devices  157 us
    psum x1, blocking collectives, on_device(): total = lax.psum(shared.astype(jnp.bfloat16), 'rep')  47.7 us
    all_to_all x1, waiting for transfers between devices, on_device(): lax.all_to_all(outgoing, 'bal', split_axis=0, concat_axis=0, tiled=True)  34.1 us
    all_to_all x1, waiting for transfers between devices, on_device(): lax.all_to_all(hot_parts, 'tab', split_axis=0, concat_axis=0, tiled=True)  15.4 us
    all_to_all x1, starting transfers between devices, on_device(): lax.all_to_all(outgoing, 'bal', split_axis=0, concat_axis=0, tiled=True)  12.1 us
    unnamed x22, local copies, waits for them, and re-layouts  9.22 us
    all_to_all x1, waiting for transfers between devices, on_device(): lax.all_to_all(cold_parts, 'tab', split_axis=0, concat_axis=0, tiled=True)  7.74 us
    dot_general x1, matrix products, on_device(): jnp.dot(balanced, proj_weight, preferred_element_type=jnp.float32)  7.54 us
  transfers between devices with their start and end apart: 4, of which 4 were waited for; matrix products, arithmetic and copies ran while one was open for 2% of the time, Pallas kernels for 0%

commit v1 on v0

v1 whole, which is shorter than its diff:
```python
import functools

import jax
import jax.numpy as jnp
from jax import lax
from jax.experimental import pallas as pl
from jax.experimental.pallas import tpu as pltpu
from jax.sharding import PartitionSpec as P

HEAD = 128
MAXLEN = 88
CAP = 96
WIN = 128
F32, BF16 = jnp.float32, jnp.bfloat16
TILE = 128


def iota(shape, dim):
    return lax.broadcasted_iota(jnp.int32, shape, dim)


def normalize(rows_in):
    center = jnp.mean(rows_in, axis=-1, keepdims=True)
    centered = rows_in - center
    deviation = jnp.mean(centered * centered, axis=-1, keepdims=True)
    return centered * lax.rsqrt(deviation + 1e-05)


def dot_nt(a, b):
    return lax.dot_general(a, b, (((1,), (1,)), ((), ())), preferred_element_type=F32)


def dot_nn(a, b):
    return jnp.dot(a, b, preferred_element_type=F32)


def flag(cond):
    return jnp.where(cond, 1.0, 0.0).astype(BF16)


def farthest_first(count):
    return sorted(range(1, count), key=lambda d: -min(d, count - d))


def layer_kernel(
    nr, nb, nt, most, chunks, gchunks,
    hot_hbm, cold_hbm, code_ref, len_ref, dest_ref, w_hbm, og_hbm,
    att_hbm, grad_ref,
    hot, cold, w, og, ogp, xsend, xrecv, bmat, smat, ysend, yrecv, tmat, bal, acc, prj, scale,
    asum, att, csend, crecv, gown, xs2, xr2, ys2, yr2, zs, zr, zo, zg,
    load_sem, xs_sem, xr_sem, ys_sem, yr_sem, cs_sem, cr_sem, xs2_sem, xr2_sem, ys2_sem, yr2_sem,
    zs_sem, zr_sem, gs_sem, gr_sem,
):
    home, model = og.shape
    nx = nt // 2
    width = model // chunks
    gwidth = model // gchunks
    heads = model // HEAD
    pair = 2 * most
    nz = zs.shape[0]
    zwidth = model // nz
    rep_id = lax.axis_index("rep")
    bal_id = lax.axis_index("bal")
    tab_id = lax.axis_index("tab")
    core = lax.rem(tab_id, 2)
    x_id = lax.div(tab_id, 2)

    loads = [
        pltpu.make_async_copy(src, dst, load_sem.at[i])
        for i, (src, dst) in enumerate(
            ((hot_hbm, hot), (cold_hbm, cold), (og_hbm, og), (w_hbm, w))
        )
    ]
    for load in loads:
        load.start()

    barrier = pltpu.get_barrier_semaphore()
    for axis, me, count in (("tab", tab_id, nt), ("bal", bal_id, nb), ("rep", rep_id, nr)):
        for d in range(1, count):
            pl.semaphore_signal(barrier, inc=1, device_id={axis: lax.rem(me + d, count)})

    loads[0].wait()
    loads[1].wait()

    @pl.loop(0, nx)
    def _(i):
        rows = pl.ds(pl.multiple_of(i * 2 * most, 16), 2 * most)
        hot_n = normalize(hot[rows, :])
        cold_n = normalize(cold[rows, :].astype(F32))
        for k in range(2):
            part = slice(k * most, (k + 1) * most)
            block = jnp.concatenate([hot_n[part], cold_n[part]], axis=0).astype(BF16)
            for c in range(chunks):
                xsend[c, 2 * i + k] = block[:, c * width : (c + 1) * width]

    pl.semaphore_wait(barrier, nt - 1 + nb - 1 + nr - 1)

    def x_copy(c, d, arriving):
        p = lax.rem(tab_id + d, nt)
        return pltpu.make_async_remote_copy(
            src_ref=xsend.at[c, p],
            dst_ref=xrecv.at[c, p if arriving else tab_id],
            send_sem=xs_sem.at[c, p],
            recv_sem=xr_sem.at[c, p if arriving else tab_id],
            device_id={"tab": p},
        )

    for c in range(chunks):
        for d in farthest_first(nt):
            x_copy(c, d, False).start()
    for c in range(chunks):
        xrecv[c, tab_id] = xsend[c, tab_id]

    start = [jnp.int32(0)] * nb
    length = [jnp.int32(0)] * nb
    run = jnp.int32(0)
    for h in range(nb):
        here = len_ref[bal_id * nb + h]
        goal = dest_ref[bal_id * nb + h]
        for b in range(nb):
            start[b] = jnp.where(goal == b, run, start[b])
            length[b] = jnp.where(goal == b, here, length[b])
        run = run + here
    in_len, in_off = [], []
    run = jnp.int32(0)
    for s in range(nb):
        got = jnp.int32(0)
        for h in range(nb):
            got = got + jnp.where(dest_ref[s * nb + h] == bal_id, len_ref[s * nb + h], 0)
        in_len.append(got)
        in_off.append(run)
        run = run + got

    codes = code_ref[...]
    flags = jnp.where(iota((2 * nt, home), 0) == codes, 1.0, 0.0)
    before = flag(iota((home, home), 0) < iota((home, home), 1))
    earlier = dot_nn(flags.astype(BF16), before)
    slot = jnp.sum(flags * earlier, axis=0, keepdims=True).astype(jnp.int32)
    tier = jnp.where(codes >= nt, 1, 0)
    place = (codes - nt * tier) * pair + tier * most + slot
    for s in range(nt):
        bmat[s * pair : (s + 1) * pair, :] = flag(iota((pair, home), 0) + s * pair == place)
    offset, position = iota((CAP, home), 0), iota((CAP, home), 1)
    for b in range(nb):
        chosen = flag((position - offset == start[b]) & (offset < length[b]))
        smat[b * CAP : (b + 1) * CAP, :] = dot_nt(chosen, bmat[...]).astype(BF16)
    row, lane = iota((home, WIN), 0), iota((home, WIN), 1)
    for s in range(nb):
        tmat[:, s * WIN : (s + 1) * WIN] = flag((row - in_off[s] == lane) & (lane < in_len[s]))
    yrecv[:, :, CAP:, :] = jnp.zeros((chunks, nb, WIN - CAP, width), BF16)

    def y_copy(c, d, arriving):
        p = lax.rem(bal_id + d, nb)
        at = p if arriving else bal_id
        return pltpu.make_async_remote_copy(
            src_ref=ysend.at[c, p],
            dst_ref=yrecv.at[c, at, pl.ds(0, CAP)],
            send_sem=ys_sem.at[c, p],
            recv_sem=yr_sem.at[c, at],
            device_id={"bal": p},
        )

    for c in range(chunks):
        for d in farthest_first(nt):
            x_copy(c, d, True).wait_recv()
        moved = dot_nn(smat[...], xrecv[c].reshape(nt * pair, width)).astype(BF16)
        ysend[c] = moved.reshape(nb, CAP, width)
        for d in farthest_first(nb):
            y_copy(c, d, False).start()
        yrecv[c, bal_id, 0:CAP] = ysend[c, bal_id]

    loads[2].wait()
    for b in range(nb):
        cols = 16 * nt
        turned = og[:, b * cols : (b + 1) * cols].T
        ogp[:, b * 16 : (b + 1) * 16, :] = turned.reshape(nt, 16, home)
    query, key = iota((TILE, 2 * TILE), 0), iota((TILE, 2 * TILE), 1)
    for i in range(home // TILE):
        at = query + i * TILE
        source = key + (i - 1) * TILE
        first = jnp.zeros_like(at)
        for s in range(1, nb):
            first = jnp.where(in_off[s] <= at, in_off[s], first)
        scale[i] = jnp.where((source <= at) & (source >= first), 0.5 * HEAD**-0.5, 0.0)

    loads[3].wait()
    early = model - width
    step = 512
    for c in range(chunks):
        for d in farthest_first(nb):
            y_copy(c, d, True).wait_recv()
        bal[:, c * width : (c + 1) * width] = dot_nn(
            tmat[...], yrecv[c].reshape(nb * WIN, width)
        ).astype(BF16)
        if c == chunks - 2:

            @pl.loop(0, 4 * model // step)
            def _(n):
                cols = pl.ds(pl.multiple_of(n * step, step), step)
                acc[:, cols] = dot_nn(bal[:, :early], w[:early, cols])

    @pl.loop(0, 4 * model // step)
    def _(n):
        cols = pl.ds(pl.multiple_of(n * step, step), step)
        half = 0.5 * (acc[:, cols] + dot_nn(bal[:, early:], w[early:, cols]))
        prj[:, cols] = (half + half * jnp.tanh(half)).astype(BF16)

    @pl.loop(0, heads)
    def _(h):
        def cols(part):
            return pl.ds(pl.multiple_of(part * model + h * HEAD, HEAD), HEAD)

        for i in range(home // TILE):
            rows = slice(i * TILE, (i + 1) * TILE)
            low = max(0, i - 1) * TILE
            keys = slice(low, (i + 1) * TILE)
            lanes = slice(2 * TILE - (i + 1) * TILE + low, 2 * TILE)
            scores = dot_nt(prj[rows, cols(2)], prj[keys, cols(3)])
            half = scores * scale[i, :, lanes]
            weights = (half + half * jnp.tanh(half)).astype(BF16)
            asum[rows, cols(0)] = dot_nn(weights, prj[keys, cols(1)])

    ln_rows = 64

    @pl.loop(0, home // ln_rows)
    def _(i):
        rows = pl.ds(pl.multiple_of(i * ln_rows, ln_rows), ln_rows)
        att[rows, :] = (normalize(asum[rows, :]) * prj[rows, :model].astype(F32)).astype(BF16)

    att_copy = pltpu.make_async_copy(att, att_hbm, load_sem.at[4])
    att_copy.start()

    def c_copy(g):
        return pltpu.make_async_remote_copy(
            src_ref=csend.at[g],
            dst_ref=crecv.at[g],
            send_sem=cs_sem.at[g],
            recv_sem=cr_sem.at[g],
            device_id={"tab": tab_id + 1 - 2 * core},
        )

    def x2_copy(g, d, arriving):
        p = lax.rem(x_id + d, nx)
        at = p if arriving else x_id
        return pltpu.make_async_remote_copy(
            src_ref=xs2.at[g, p],
            dst_ref=xr2.at[g, at],
            send_sem=xs2_sem.at[g, p],
            recv_sem=xr2_sem.at[g, at],
            device_id={"tab": 2 * p + core},
        )

    def y2_copy(g, d, arriving):
        p = lax.rem(bal_id + d, nb)
        at = p if arriving else bal_id
        return pltpu.make_async_remote_copy(
            src_ref=ys2.at[g, p],
            dst_ref=yr2.at[g, at],
            send_sem=ys2_sem.at[g, p],
            recv_sem=yr2_sem.at[g, at],
            device_id={"bal": p},
        )

    for g in range(gchunks):
        cols = slice(g * gwidth, (g + 1) * gwidth)
        for x in range(nx):
            csend[g, x] = dot_nn(ogp[2 * x + 1 - core], att[:, cols]).astype(BF16)
        c_copy(g).start()
    for g in range(gchunks):
        cols = slice(g * gwidth, (g + 1) * gwidth)
        for x in range(nx):
            gown[g, x] = dot_nn(ogp[2 * x + core], att[:, cols])
    for g in range(gchunks):
        c_copy(g).wait_recv()
        for x in range(nx):
            both = gown[g, x] + crecv[g, x].astype(F32)
            gown[g, x] = both
            xs2[g, x] = both.astype(BF16)
        for d in farthest_first(nx):
            x2_copy(g, d, False).start()
    for g in range(gchunks):
        total = gown[g, x_id]
        for d in farthest_first(nx):
            x2_copy(g, d, True).wait_recv()
            total = total + xr2[g, lax.rem(x_id + d, nx)].astype(F32)
        gown[g, x_id] = total
        ys2[g] = total.astype(BF16).reshape(nb, 16, gwidth)
        for d in farthest_first(nb):
            y2_copy(g, d, False).start()
    for g in range(gchunks):
        own_rows = pl.ds(pl.multiple_of(bal_id * 16, 16), 16)
        total = gown[g, x_id, own_rows, :]
        for d in farthest_first(nb):
            y2_copy(g, d, True).wait_recv()
            total = total + yr2[g, lax.rem(bal_id + d, nb)].astype(F32)
        total = total.astype(BF16)
        for j in range(gwidth // zwidth):
            zs[g * (gwidth // zwidth) + j] = total[:, j * zwidth : (j + 1) * zwidth]

    def z_send(j):
        return pltpu.make_async_remote_copy(
            src_ref=zs.at[j],
            dst_ref=zr.at[rep_id],
            send_sem=zs_sem.at[j],
            recv_sem=zr_sem.at[rep_id],
            device_id={"rep": j},
        )

    def z_arrive(p):
        return pltpu.make_async_remote_copy(
            src_ref=zs.at[0],
            dst_ref=zr.at[p],
            send_sem=zs_sem.at[0],
            recv_sem=zr_sem.at[p],
            device_id={"rep": p},
        )

    def g_send(d):
        p = lax.rem(rep_id + d, nr)
        return pltpu.make_async_remote_copy(
            src_ref=zo,
            dst_ref=zg.at[rep_id],
            send_sem=gs_sem.at[p],
            recv_sem=gr_sem.at[rep_id],
            device_id={"rep": p},
        )

    def g_arrive(j):
        return pltpu.make_async_remote_copy(
            src_ref=zo,
            dst_ref=zg.at[j],
            send_sem=gs_sem.at[0],
            recv_sem=gr_sem.at[j],
            device_id={"rep": j},
        )

    for j in range(nz):

        @pl.when(rep_id != j)
        def _():
            z_send(j).start()

    @pl.when(rep_id < nz)
    def _():
        total = zs[rep_id].astype(F32)
        for d in range(1, nr):
            p = lax.rem(rep_id + d, nr)
            z_arrive(p).wait_recv()
            total = total + zr[p].astype(F32)
        zo[...] = total.astype(BF16)
        for d in farthest_first(nr):
            g_send(d).start()
        zg[rep_id] = total.astype(BF16)

    for j in range(nz):

        @pl.when(rep_id != j)
        def _():
            g_arrive(j).wait_recv()

        grad_ref[:, j * zwidth : (j + 1) * zwidth] = zg[j]

    for c in range(chunks):
        for d in range(1, nt):
            x_copy(c, d, False).wait_send()
        for d in range(1, nb):
            y_copy(c, d, False).wait_send()
    for g in range(gchunks):
        c_copy(g).wait_send()
        for d in range(1, nx):
            x2_copy(g, d, False).wait_send()
        for d in range(1, nb):
            y2_copy(g, d, False).wait_send()
    for j in range(nz):

        @pl.when(rep_id != j)
        def _():
            z_send(j).wait_send()

    @pl.when(rep_id < nz)
    def _():
        for d in range(1, nr):
            g_send(d).wait_send()

    att_copy.wait()


def on_device(sizes, hot_rows, cold_rows, row_source, lengths, destination, proj_weight, out_grad):
    nr, nb, nt = sizes
    home, model = out_grad.shape
    most = hot_rows.shape[0] // nt
    chunks = 4 if model >= 1024 else 2
    gchunks = 2
    nx, width, gwidth, pair = nt // 2, model // chunks, model // gchunks, 2 * most
    nz = min(nr, 8)
    vmem = pltpu.VMEM
    dma = pltpu.SemaphoreType.DMA
    scratch = [
        vmem(hot_rows.shape, F32),
        vmem(cold_rows.shape, BF16),
        vmem(proj_weight.shape, BF16),
        vmem(out_grad.shape, BF16),
        vmem((nt, nb * 16, home), BF16),
        vmem((chunks, nt, pair, width), BF16),
        vmem((chunks, nt, pair, width), BF16),
        vmem((nt * pair, home), BF16),
        vmem((nb * CAP, nt * pair), BF16),
        vmem((chunks, nb, CAP, width), BF16),
        vmem((chunks, nb, WIN, width), BF16),
        vmem((home, nb * WIN), BF16),
        vmem((home, model), BF16),
        vmem((home, 4 * model), F32),
        vmem((home, 4 * model), BF16),
        vmem((home // TILE, TILE, 2 * TILE), F32),
        vmem((home, model), F32),
        vmem((home, model), BF16),
        vmem((gchunks, nx, nb * 16, gwidth), BF16),
        vmem((gchunks, nx, nb * 16, gwidth), BF16),
        vmem((gchunks, nx, nb * 16, gwidth), F32),
        vmem((gchunks, nx, nb * 16, gwidth), BF16),
        vmem((gchunks, nx, nb * 16, gwidth), BF16),
        vmem((gchunks, nb, 16, gwidth), BF16),
        vmem((gchunks, nb, 16, gwidth), BF16),
        vmem((nz, 16, model // nz), BF16),
        vmem((nr, 16, model // nz), BF16),
        vmem((16, model // nz), BF16),
        vmem((nz, 16, model // nz), BF16),
        dma((5,)),
        dma((chunks, nt)),
        dma((chunks, nt)),
        dma((chunks, nb)),
        dma((chunks, nb)),
        dma((gchunks,)),
        dma((gchunks,)),
        dma((gchunks, nx)),
        dma((gchunks, nx)),
        dma((gchunks, nb)),
        dma((gchunks, nb)),
        dma((nz,)),
        dma((nr,)),
        dma((nr,)),
        dma((nz,)),
    ]
    hbm = pl.BlockSpec(memory_space=pl.ANY)
    here = pl.BlockSpec(memory_space=pltpu.VMEM)
    scalar = pl.BlockSpec(memory_space=pltpu.SMEM)
    return pl.pallas_call(
        functools.partial(layer_kernel, nr, nb, nt, most, chunks, gchunks),
        out_shape=(
            jax.ShapeDtypeStruct((home, model), BF16),
            jax.ShapeDtypeStruct((model // (nb * nt), model), BF16),
        ),
        in_specs=[hbm, hbm, here, scalar, scalar, hbm, hbm],
        out_specs=(hbm, here),
        scratch_shapes=scratch,
        compiler_params=pltpu.CompilerParams(
            collective_id=0, has_side_effects=True, vmem_limit_bytes=58 * 1024 * 1024
        ),
    )(
        hot_rows,
        cold_rows,
        row_source.reshape(1, home),
        lengths.reshape(-1),
        destination.reshape(-1),
        proj_weight,
        out_grad,
    )


def solution(mesh):
    sizes = tuple(mesh.shape[axis] for axis in ("rep", "bal", "tab"))
    in_specs = (
        P(("rep", "bal", "tab"), None),
        P(("rep", "bal", "tab"), None),
        P(("rep", "bal", "tab"), None),
        P("rep", None, "tab", None),
        P("rep", None, "tab", None),
        P(),
        P(("rep", "bal", "tab"), None),
    )
    out_specs = (P(("rep", "bal", "tab"), None), P(("bal", "tab"), None))
    return jax.shard_map(
        functools.partial(on_device, sizes),
        mesh=mesh,
        in_specs=in_specs,
        out_specs=out_specs,
        check_vma=False,
    )
```

time: 348 us -> 116 us (0.33)
  the two profiles are of different devices: /device:TPU:16 before, /device:TPU:1 now
where the time goes in v1:
time: 116 us; the launch traced here: 115 us
  Pallas kernels  107 us (92%)
  local copies, waits for them, and re-layouts  5.13 us (4%)
  other arithmetic  2.69 us (2%)
    pallas_call x1, Pallas kernels, on_device(): pl.pallas_call(functools.partial(layer_kernel, nr, nb, nt, most, chunks,...  107 us
    unnamed x3, local copies, waits for them, and re-layouts  3.95 us
    unnamed x2, other arithmetic  2.69 us

profile of v1, /device:TPU:1, one launch (start us, length us, event | category | flops | bytes accessed | tf_op | source)
XLA Modules:
  0.0 115.2 jit_solution(16396941244573541495)
XLA Ops:
  0.6 0.5 broadcast.6
  1.1 1.3 %reduce.6 = s32[8,8]{1,0:T(8,128)S(1)} reduce(s32[1,8,1,8]{3,2,1,0:T(1,128)} %param.10, s32[]{:T(128)} %broadcast.6), dimensions={0,2}, to_apply=%param.10.reduce_sub_computation.3 | reduce | bytes 516 | tf_op args[3]
  2.5 0.6 reshape.14.len_ref
  3.1 1.3 %reduce.7 = s32[8,8]{1,0:T(8,128)S(1)} reduce(s32[1,8,1,8]{3,2,1,0:T(1,128)} %param.11, s32[]{:T(128)} %broadcast.6), dimensions={0,2}, to_apply=%param.11.reduce_sub_computation.3 | reduce | bytes 516 | tf_op args[4]
  4.4 0.6 reshape.15.dest_ref
  5.0 106.7 %shard_map.86 = (bf16[384,1024]{1,0:T(8,128)(2,1)}, bf16[16,1024]{1,0:T(8,128)(2,1)}) custom-call(f32[320,1024]{1,0:T(8,128)} %hot_hbm.1, bf16[320,1024]{1,0:T(8,128)(2,1)} %cold_hbm.1, s32[1,384]{1,0:T(1,128)} %bitcast.1, s32[64]{0:T(128)} %reshape.14.len_ref, s32[64]{0:T(128)} %reshape.15.dest_ref, bf16[1024,4096]{1,0:T(8,128)(2,1)} %w_hbm.1, ...), custom_call_target="tpu_custom_call" | custom-call | tf_op jit(solution)/shard_map/pallas_call | solution.py:447
  111.7 2.1 %copy.11 = bf16[384,1024]{1,0:T(8,128)(2,1)} copy(bf16[384,1024]{1,0:T(8,128)(2,1)} %get-tuple-element.4) | data formatting | bytes 1572864
  113.8 1.4 %copy.12 = bf16[16,1024]{1,0:T(8,128)(2,1)} copy(bf16[16,1024]{1,0:T(8,128)(2,1)} %get-tuple-element.5) | data formatting | bytes 65536

commit v2 on v0

v2 whole, which is shorter than its diff:
```python
import functools

import jax
import jax.numpy as jnp
from jax import lax
from jax.experimental import pallas as pl
from jax.experimental.pallas import tpu as pltpu
from jax.sharding import PartitionSpec as P

HEAD = 128
MAXLEN = 88
WIN = 96
F32, BF16 = jnp.float32, jnp.bfloat16
TILE = 128


def iota(shape, dim):
    return lax.broadcasted_iota(jnp.int32, shape, dim)


def normalize(rows_in):
    center = jnp.mean(rows_in, axis=-1, keepdims=True)
    centered = rows_in - center
    deviation = jnp.mean(centered * centered, axis=-1, keepdims=True)
    return centered * lax.rsqrt(deviation + 1e-05)


def dot_nt(a, b):
    return lax.dot_general(a, b, (((1,), (1,)), ((), ())), preferred_element_type=F32)


def dot_nn(a, b):
    return jnp.dot(a, b, preferred_element_type=F32)


def flag(cond):
    return jnp.where(cond, 1.0, 0.0).astype(BF16)


def farthest_first(count):
    return sorted(range(1, count), key=lambda d: -min(d, count - d))


def layer_kernel(
    nr, nb, nt, most, widths, ahead, gorder,
    hot_hbm, cold_hbm, code_hbm, len_hbm, dest_hbm, w_hbm, og_hbm,
    att_hbm, grad_ref,
    xsend, xrecv, ysend, yrecv,
    code_ref, len_ref, dest_ref,
    hot, cold, w, og, ogp, ogr, bmat, smat, spread, tmat, bal, acc, prj, scale,
    asum, att, attr, gown, xs2, xr2, ys2, yr2, ybs, ybr, xbs, xbr, zs, zr, zo, zg,
    load_sem, xs_sem, xr_sem, ys_sem, yr_sem, os_sem, or_sem, as_sem, ar_sem,
    xs2_sem, xr2_sem, ys2_sem, yr2_sem, ybs_sem, ybr_sem, xbs_sem, xbr_sem,
    zs_sem, zr_sem, gs_sem, gr_sem,
):
    home, model = og.shape
    nx = nt // 2
    chunks = len(widths)
    firsts = [sum(widths[:c]) for c in range(chunks)]
    tiles = home // TILE
    heads = model // HEAD
    pair = 2 * most
    nz = zs.shape[0]
    zwidth = model // nz
    gwidth = model // len(gorder)
    rep_id = lax.axis_index("rep")
    bal_id = lax.axis_index("bal")
    tab_id = lax.axis_index("tab")
    core = lax.rem(tab_id, 2)
    x_id = lax.div(tab_id, 2)
    sibling = tab_id + 1 - 2 * core

    loads = [
        pltpu.make_async_copy(src, dst, load_sem.at[i])
        for i, (src, dst) in enumerate(
            (
                (hot_hbm, hot), (cold_hbm, cold), (code_hbm, code_ref), (len_hbm, len_ref),
                (dest_hbm, dest_ref), (og_hbm, og), (w_hbm, w),
            )
        )
    ]
    att_copy = pltpu.make_async_copy(att, att_hbm, load_sem.at[7])

    def remote(src, dst, send, recv, axis, peer):
        return pltpu.make_async_remote_copy(
            src_ref=src, dst_ref=dst, send_sem=send, recv_sem=recv, device_id={axis: peer}
        )

    def exchange(src, dst, send, recv, axis, me, count, d, c, arriving):
        p = lax.rem(me + d, count)
        at = p if arriving else me
        peer = 2 * p + core if axis == "x" else p
        return remote(
            src.at[p], dst.at[at], send.at[c, p], recv.at[c, at], "tab" if axis == "x" else axis, peer
        )

    def x_copy(c, d, arriving=False):
        return exchange(xsend[c], xrecv[c], xs_sem, xr_sem, "tab", tab_id, nt, d, c, arriving)

    def y_copy(c, d, arriving=False):
        return exchange(ysend[c], yrecv[c], ys_sem, yr_sem, "bal", bal_id, nb, d, c, arriving)

    def x2_copy(a, d, arriving=False):
        return exchange(
            xs2.at[a], xr2.at[a], xs2_sem, xr2_sem, "x", x_id, nx, d, a, arriving
        )

    def y2_copy(a, d, arriving=False):
        return exchange(
            ys2.at[a], yr2.at[a], ys2_sem, yr2_sem, "bal", bal_id, nb, d, a, arriving
        )

    def yb_copy(a, d, arriving=False):
        return exchange(
            ybs.at[a], ybr.at[a], ybs_sem, ybr_sem, "bal", bal_id, nb, d, a, arriving
        )

    def xb_copy(a, d, arriving=False):
        return exchange(
            xbs.at[a], xbr.at[a], xbs_sem, xbr_sem, "x", x_id, nx, d, a, arriving
        )

    def o_copy(x):
        return remote(
            ogp.at[2 * x + 1 - core], ogr.at[x], os_sem.at[x], or_sem.at[x], "tab", sibling
        )

    def a_copy(i):
        rows = pl.ds(i * TILE, TILE)
        return remote(att.at[rows], attr.at[rows], as_sem.at[i], ar_sem.at[i], "tab", sibling)

    def z_copy(j):
        return remote(zs.at[j], zr.at[rep_id], zs_sem.at[j], zr_sem.at[rep_id], "rep", j)

    def z_arrive(p):
        return remote(zs.at[0], zr.at[p], zs_sem.at[0], zr_sem.at[p], "rep", p)

    def g_copy(d):
        p = lax.rem(rep_id + d, nr)
        return remote(zo, zg.at[rep_id], gs_sem.at[p], gr_sem.at[rep_id], "rep", p)

    def g_arrive(j):
        return remote(zo, zg.at[j], gs_sem.at[0], gr_sem.at[j], "rep", j)

    def load_and_greet():
        for load in loads[:5]:
            load.start()
        barrier = pltpu.get_barrier_semaphore()
        for axis, me, count in (("tab", tab_id, nt), ("bal", bal_id, nb), ("rep", rep_id, nr)):
            for d in range(1, count):
                pl.semaphore_signal(barrier, inc=1, device_id={axis: lax.rem(me + d, count)})
        loads[0].wait()
        loads[1].wait()
        loads[5].start()
        loads[6].start()

    def normalize_rows():
        @pl.loop(0, nx)
        def _(i):
            rows = pl.ds(pl.multiple_of(i * 2 * most, 16), 2 * most)
            hot_n = normalize(hot[rows, :])
            cold_n = normalize(cold[rows, :].astype(F32))
            for k in range(2):
                part = slice(k * most, (k + 1) * most)
                block = jnp.concatenate([hot_n[part], cold_n[part]], axis=0).astype(BF16)
                for c in range(chunks):
                    xsend[c][2 * i + k] = block[:, firsts[c] : firsts[c] + widths[c]]

    def greeted():
        pl.semaphore_wait(pltpu.get_barrier_semaphore(), nt - 1 + nb - 1 + nr - 1)

    def x_start(c):
        for d in farthest_first(nt):
            x_copy(c, d).start()

    def history_bounds():
        for load in loads[2:5]:
            load.wait()
        start = [jnp.int32(0)] * nb
        length = [jnp.int32(0)] * nb
        run = jnp.int32(0)
        for h in range(nb):
            here = len_ref[0, bal_id, 0, h]
            goal = dest_ref[0, bal_id, 0, h]
            for b in range(nb):
                start[b] = jnp.where(goal == b, run, start[b])
                length[b] = jnp.where(goal == b, here, length[b])
            run = run + here
        in_off = []
        run = jnp.int32(0)
        for s in range(nb):
            in_off.append(run)
            for h in range(nb):
                run = run + jnp.where(dest_ref[0, s, 0, h] == bal_id, len_ref[0, s, 0, h], 0)
        return start, length, in_off

    def placements(start, length, in_off):
        codes = code_ref[...]
        flags = jnp.where(iota((2 * nt, home), 0) == codes, 1.0, 0.0)
        before = flag(iota((home, home), 0) < iota((home, home), 1))
        earlier = dot_nn(flags.astype(BF16), before)
        slot = jnp.sum(flags * earlier, axis=0, keepdims=True).astype(jnp.int32)
        tier = jnp.where(codes >= nt, 1, 0)
        place = (codes - nt * tier) * pair + tier * most + slot
        bmat[...] = flag(iota((nt * pair, home), 0) == place)
        gap = iota((MAXLEN, home), 1) - iota((MAXLEN, home), 0)
        offset = iota((MAXLEN, home), 0)
        for b in range(0, nb, 2):
            chosen = jnp.concatenate(
                [
                    jnp.where((gap == start[k]) & (offset < length[k]), 1.0, 0.0)
                    for k in (b, b + 1)
                ],
                axis=0,
            ).astype(BF16)
            smat[b * MAXLEN : (b + 2) * MAXLEN, :] = dot_nt(chosen, bmat[...]).astype(BF16)
        row = iota((home, WIN), 0)
        moved = jnp.zeros_like(row)
        for s in range(1, nb):
            moved = jnp.where(row >= in_off[s], s * WIN - in_off[s], moved)
        source = (row + moved)[:, :1]
        tmat[...] = flag(iota((home, nb * WIN), 1) == source)

    def x_to_y(c):
        for d in farthest_first(nt):
            x_copy(c, d, True).wait_recv()
        if c + ahead < chunks:
            x_start(c + ahead)
        xrecv[c][tab_id] = xsend[c][tab_id]
        width = widths[c]
        out = dot_nn(smat[...], xrecv[c][...].reshape(nt * pair, width))
        for b in range(nb):
            block = out[b * MAXLEN : (b + 1) * MAXLEN]
            if width > 128:
                block = jnp.concatenate([block[:, : width // 2], block[:, width // 2 :]], axis=0)
            else:
                block = jnp.concatenate([block, jnp.zeros((WIN - MAXLEN, width), F32)], axis=0)
            ysend[c][b] = block.astype(BF16)
        for d in farthest_first(nb):
            y_copy(c, d).start()
        yrecv[c][bal_id] = ysend[c][bal_id]

    def y_in(c):
        width = widths[c]
        for d in farthest_first(nb):
            y_copy(c, d, True).wait_recv()
        if width > 128:
            for s in range(nb):
                block = yrecv[c][s].astype(F32)
                block = jnp.concatenate([block[:MAXLEN], block[MAXLEN:]], axis=1)
                block = jnp.concatenate([block, jnp.zeros((WIN - MAXLEN, width), F32)], axis=0)
                spread[s * WIN : (s + 1) * WIN, :width] = block.astype(BF16)
            arrived = spread[:, :width]
        else:
            arrived = yrecv[c][...].reshape(nb * WIN, width)
        bal[:, firsts[c] : firsts[c] + width] = dot_nn(tmat[...], arrived).astype(BF16)

    def turn_out_grad():
        loads[5].wait()
        for b in range(nb):
            cols = 16 * nt
            turned = og[:, b * cols : (b + 1) * cols].T
            ogp[:, b * 16 : (b + 1) * 16, :] = turned.reshape(nt, 16, home)
        for x in range(nx):
            o_copy(x).start()

    def mask_scale(in_off):
        query, key = iota((TILE, 2 * TILE), 0), iota((TILE, 2 * TILE), 1)
        for i in range(tiles):
            at = query + i * TILE
            source = key + (i - 1) * TILE
            first = jnp.zeros_like(at)
            for s in range(1, nb):
                first = jnp.where(in_off[s] <= at, in_off[s], first)
            scale[i] = jnp.where((source <= at) & (source >= first), 0.5 * HEAD**-0.5, 0.0)

    step = 512
    early = firsts[-1]

    def project_early():
        loads[6].wait()

        @pl.loop(0, 4 * model // step)
        def _(n):
            cols = pl.ds(pl.multiple_of(n * step, step), step)
            acc[:, cols] = dot_nn(bal[:, :early], w[:early, cols])

    def project_late():
        @pl.loop(0, 4 * model // step)
        def _(n):
            cols = pl.ds(pl.multiple_of(n * step, step), step)
            half = 0.5 * (acc[:, cols] + dot_nn(bal[:, early:], w[early:, cols]))
            prj[:, cols] = (half + half * jnp.tanh(half)).astype(BF16)

    def attend(i):
        rows = slice(i * TILE, (i + 1) * TILE)
        low = max(0, i - 1) * TILE
        keys = slice(low, (i + 1) * TILE)
        lanes = slice(2 * TILE - (i + 1) * TILE + low, 2 * TILE)

        @pl.loop(0, heads // 2)
        def _(pair_of_heads):
            for k in range(2):
                def cols(part):
                    at = part * model + (pair_of_heads * 2 + k) * HEAD
                    return pl.ds(pl.multiple_of(at, HEAD), HEAD)

                scores = dot_nt(prj[rows, cols(2)], prj[keys, cols(3)])
                half = scores * scale[i, :, lanes]
                weights = (half + half * jnp.tanh(half)).astype(BF16)
                asum[rows, cols(0)] = dot_nn(weights, prj[keys, cols(1)])

    def gate(i):
        rows = slice(i * TILE, (i + 1) * TILE)
        att[rows, :] = (normalize(asum[rows, :]) * prj[rows, :model].astype(F32)).astype(BF16)

    def partial(x, cols):
        return dot_nn(ogp[2 * x + core], att[:, cols]) + dot_nn(ogr[x], attr[:, cols])

    def columns(g):
        return slice(g * gwidth, (g + 1) * gwidth)

    groups = []
    for g, kind in enumerate(gorder):
        groups.append((kind, gorder[:g].count(kind)))

    def grad_start(g):
        kind, a = groups[g]
        if kind == "A":
            for d in farthest_first(nx) + [0]:
                x = lax.rem(x_id + d, nx)
                part = partial(x, columns(g))
                if d:
                    xs2[a, x] = part.astype(BF16)
                    x2_copy(a, d).start()
                else:
                    gown[a] = part
        else:
            for x in range(nx):
                part = partial(x, columns(g)).astype(BF16)
                ybs[a, :, x * 16 : (x + 1) * 16, :] = part.reshape(nb, 16, gwidth)
            for d in farthest_first(nb):
                yb_copy(a, d).start()

    def grad_turn(g):
        kind, a = groups[g]
        if kind == "A":
            total = gown[a]
            for d in farthest_first(nx):
                x2_copy(a, d, True).wait_recv()
                total = total + xr2[a, lax.rem(x_id + d, nx)].astype(F32)
            ys2[a] = total.astype(BF16).reshape(nb, 16, gwidth)
            for d in farthest_first(nb):
                y2_copy(a, d).start()
        else:
            total = ybs[a, bal_id].astype(F32)
            for d in farthest_first(nb):
                yb_copy(a, d, True).wait_recv()
                total = total + ybr[a, lax.rem(bal_id + d, nb)].astype(F32)
            xbs[a] = total.astype(BF16).reshape(nx, 16, gwidth)
            for d in farthest_first(nx):
                xb_copy(a, d).start()

    def grad_end(g):
        kind, a = groups[g]
        if kind == "A":
            total = ys2[a, bal_id].astype(F32)
            for d in farthest_first(nb):
                y2_copy(a, d, True).wait_recv()
                total = total + yr2[a, lax.rem(bal_id + d, nb)].astype(F32)
        else:
            total = xbs[a, x_id].astype(F32)
            for d in farthest_first(nx):
                xb_copy(a, d, True).wait_recv()
                total = total + xbr[a, lax.rem(x_id + d, nx)].astype(F32)
        total = total.astype(BF16)
        for k in range(gwidth // zwidth):
            j = g * (gwidth // zwidth) + k
            zs[j] = total[:, k * zwidth : (k + 1) * zwidth]

            @pl.when(rep_id != j)
            def _():
                z_copy(j).start()

    def grad_spread():
        @pl.when(rep_id < nz)
        def _():
            total = zs[rep_id].astype(F32)
            for d in range(1, nr):
                p = lax.rem(rep_id + d, nr)
                z_arrive(p).wait_recv()
                total = total + zr[p].astype(F32)
            zo[...] = total.astype(BF16)
            for d in farthest_first(nr):
                g_copy(d).start()
            zg[rep_id] = total.astype(BF16)

        for j in range(nz):

            @pl.when(rep_id != j)
            def _():
                g_arrive(j).wait_recv()

            grad_ref[:, j * zwidth : (j + 1) * zwidth] = zg[j]

    def all_sent():
        for c in range(chunks):
            for d in range(1, nt):
                x_copy(c, d).wait_send()
            for d in range(1, nb):
                y_copy(c, d).wait_send()
        for x in range(nx):
            o_copy(x).wait_send()
        for i in range(tiles):
            a_copy(i).wait_send()
        for kind, a in groups:
            for d in range(1, nx):
                (x2_copy if kind == "A" else xb_copy)(a, d).wait_send()
            for d in range(1, nb):
                (y2_copy if kind == "A" else yb_copy)(a, d).wait_send()
        for j in range(nz):

            @pl.when(rep_id != j)
            def _():
                z_copy(j).wait_send()

        @pl.when(rep_id < nz)
        def _():
            for d in range(1, nr):
                g_copy(d).wait_send()

    load_and_greet()
    normalize_rows()
    greeted()
    for c in range(min(ahead, chunks)):
        x_start(c)
    start, length, in_off = history_bounds()
    placements(start, length, in_off)
    for c in range(chunks):
        x_to_y(c)
    turn_out_grad()
    mask_scale(in_off)
    for c in range(chunks - 1):
        y_in(c)
    project_early()
    y_in(chunks - 1)
    project_late()
    for i in range(tiles):
        attend(i)
        gate(i)
        a_copy(i).start()
    att_copy.start()
    for x in range(nx):
        o_copy(x).wait_recv()
    for i in range(tiles):
        a_copy(i).wait_recv()
    for g in range(len(gorder)):
        grad_start(g)
    for g in range(len(gorder)):
        grad_turn(g)
    for g in range(len(gorder)):
        grad_end(g)
    grad_spread()
    all_sent()
    att_copy.wait()


def on_device(sizes, hot_rows, cold_rows, row_source, lengths, destination, proj_weight, out_grad):
    nr, nb, nt = sizes
    home, model = out_grad.shape
    most = hot_rows.shape[0] // nt
    widths = (128, 256, 256, 256, 128)
    ahead = 2
    gorder = "BAAA"
    chunks, groups = len(widths), len(gorder)
    acount, bcount = gorder.count("A"), gorder.count("B")
    nx, gwidth, pair = nt // 2, model // groups, 2 * most
    nz = min(nr, 8)
    vmem = pltpu.VMEM
    dma = pltpu.SemaphoreType.DMA

    def y_block(width):
        return (2 * MAXLEN, width // 2) if width > 128 else (WIN, width)

    x_parts = [vmem((nt, pair, width), BF16) for width in widths]
    y_parts = [vmem((nb, *y_block(width)), BF16) for width in widths]
    scratch = [
        x_parts,
        x_parts,
        y_parts,
        y_parts,
        vmem((1, home), jnp.int32),
        pltpu.SMEM(lengths.shape, jnp.int32),
        pltpu.SMEM(destination.shape, jnp.int32),
        vmem(hot_rows.shape, F32),
        vmem(cold_rows.shape, BF16),
        vmem(proj_weight.shape, BF16),
        vmem(out_grad.shape, BF16),
        vmem((nt, nb * 16, home), BF16),
        vmem((nx, nb * 16, home), BF16),
        vmem((nt * pair, home), BF16),
        vmem((nb * MAXLEN, nt * pair), BF16),
        vmem((nb * WIN, max(widths)), BF16),
        vmem((home, nb * WIN), BF16),
        vmem((home, model), BF16),
        vmem((home, 4 * model), F32),
        vmem((home, 4 * model), BF16),
        vmem((home // TILE, TILE, 2 * TILE), F32),
        vmem((home, model), F32),
        vmem((home, model), BF16),
        vmem((home, model), BF16),
        vmem((acount, nb * 16, gwidth), F32),
        vmem((acount, nx, nb * 16, gwidth), BF16),
        vmem((acount, nx, nb * 16, gwidth), BF16),
        vmem((acount, nb, 16, gwidth), BF16),
        vmem((acount, nb, 16, gwidth), BF16),
        vmem((bcount, nb, nx * 16, gwidth), BF16),
        vmem((bcount, nb, nx * 16, gwidth), BF16),
        vmem((bcount, nx, 16, gwidth), BF16),
        vmem((bcount, nx, 16, gwidth), BF16),
        vmem((nz, 16, model // nz), BF16),
        vmem((nr, 16, model // nz), BF16),
        vmem((16, model // nz), BF16),
        vmem((nz, 16, model // nz), BF16),
        dma((8,)),
        dma((chunks, nt)),
        dma((chunks, nt)),
        dma((chunks, nb)),
        dma((chunks, nb)),
        dma((nx,)),
        dma((nx,)),
        dma((home // TILE,)),
        dma((home // TILE,)),
        dma((acount, nx)),
        dma((acount, nx)),
        dma((acount, nb)),
        dma((acount, nb)),
        dma((bcount, nb)),
        dma((bcount, nb)),
        dma((bcount, nx)),
        dma((bcount, nx)),
        dma((nz,)),
        dma((nr,)),
        dma((nr,)),
        dma((nz,)),
    ]
    hbm = pl.BlockSpec(memory_space=pl.ANY)
    return pl.pallas_call(
        functools.partial(layer_kernel, nr, nb, nt, most, widths, ahead, gorder),
        out_shape=(
            jax.ShapeDtypeStruct((home, model), BF16),
            jax.ShapeDtypeStruct((model // (nb * nt), model), BF16),
        ),
        in_specs=[hbm] * 7,
        out_specs=(hbm, pl.BlockSpec(memory_space=pltpu.VMEM)),
        scratch_shapes=scratch,
        compiler_params=pltpu.CompilerParams(
            collective_id=0, has_side_effects=True, vmem_limit_bytes=58 * 1024 * 1024
        ),
    )(
        hot_rows,
        cold_rows,
        row_source.reshape(1, home),
        lengths,
        destination,
        proj_weight,
        out_grad,
    )


def solution(mesh):
    sizes = tuple(mesh.shape[axis] for axis in ("rep", "bal", "tab"))
    in_specs = (
        P(("rep", "bal", "tab"), None),
        P(("rep", "bal", "tab"), None),
        P(("rep", "bal", "tab"), None),
        P("rep", None, "tab", None),
        P("rep", None, "tab", None),
        P(),
        P(("rep", "bal", "tab"), None),
    )
    out_specs = (P(("rep", "bal", "tab"), None), P(("bal", "tab"), None))
    return jax.shard_map(
        functools.partial(on_device, sizes),
        mesh=mesh,
        in_specs=in_specs,
        out_specs=out_specs,
        check_vma=False,
    )
```

time: 348 us -> 105 us (0.30)
  the two profiles are of different devices: /device:TPU:16 before, /device:TPU:1 now
where the time goes in v2:
time: 105 us; the launch traced here: 104 us
  Pallas kernels  100 us (95%)
  local copies, waits for them, and re-layouts  3.44 us (3%)
    pallas_call x1, Pallas kernels, on_device(): pl.pallas_call(functools.partial(layer_kernel, nr, nb, nt, most, widths,...  100 us
    unnamed x2, local copies, waits for them, and re-layouts  3.44 us

profile of v2, /device:TPU:1, one launch (start us, length us, event | category | flops | bytes accessed | tf_op | source)
XLA Modules:
  0.0 104.2 jit_solution(1131594350367856617)
XLA Ops:
  0.6 100.1 %shard_map.86 = (bf16[384,1024]{1,0:T(8,128)(2,1)}, bf16[16,1024]{1,0:T(8,128)(2,1)}) custom-call(f32[320,1024]{1,0:T(8,128)} %hot_hbm.1, bf16[320,1024]{1,0:T(8,128)(2,1)} %cold_hbm.1, s32[1,384]{1,0:T(1,128)} %bitcast.1, s32[1,8,1,8]{3,2,1,0:T(1,128)} %len_hbm.1, s32[1,8,1,8]{3,2,1,0:T(1,128)} %dest_hbm.1, bf16[1024,4096]{1,0:T(8,128)(2,1)} %w_hbm.1, ...), custom_call_target="tpu_custom_call" | custom-call | tf_op jit(solution)/shard_map/pallas_call | solution.py:548
  100.8 2.1 %copy.11 = bf16[384,1024]{1,0:T(8,128)(2,1)} copy(bf16[384,1024]{1,0:T(8,128)(2,1)} %get-tuple-element.4) | data formatting | bytes 1572864
  102.8 1.4 %copy.12 = bf16[16,1024]{1,0:T(8,128)(2,1)} copy(bf16[16,1024]{1,0:T(8,128)(2,1)} %get-tuple-element.5) | data formatting | bytes 65536

commit v3 on v2

--- a/solution.py
+++ b/solution.py
@@ -42,16 +42,15 @@
 
 
 def layer_kernel(
-    nr, nb, nt, most, widths, ahead, gorder,
+    nr, nb, nt, most, widths, ahead, groups,
     hot_hbm, cold_hbm, code_hbm, len_hbm, dest_hbm, w_hbm, og_hbm,
     att_hbm, grad_ref,
-    xsend, xrecv, ysend, yrecv,
+    xsend, xrecv, ysend, yrecv, first_out, first_in, next_out, next_in, whole_out, whole_in,
     code_ref, len_ref, dest_ref,
     hot, cold, w, og, ogp, ogr, bmat, smat, spread, tmat, bal, acc, prj, scale,
-    asum, att, attr, gown, xs2, xr2, ys2, yr2, ybs, ybr, xbs, xbr, zs, zr, zo, zg,
+    asum, att, attr, zs, zr, zo, zg,
     load_sem, xs_sem, xr_sem, ys_sem, yr_sem, os_sem, or_sem, as_sem, ar_sem,
-    xs2_sem, xr2_sem, ys2_sem, yr2_sem, ybs_sem, ybr_sem, xbs_sem, xbr_sem,
-    zs_sem, zr_sem, gs_sem, gr_sem,
+    fs_sem, fr_sem, ns_sem, nr_sem, ws_sem, wr_sem, zs_sem, zr_sem, gs_sem, gr_sem, hop_sem,
 ):
     home, model = og.shape
     nx = nt // 2
@@ -60,9 +59,13 @@
     tiles = home // TILE
     heads = model // HEAD
     pair = 2 * most
-    nz = zs.shape[0]
-    zwidth = model // nz
-    gwidth = model // len(gorder)
+    gcount = len(groups)
+    gfirsts = [sum(width for _, width, _ in groups[:g]) for g in range(gcount)]
+    direct = [g for g in range(gcount) if groups[g][2]]
+    owned = [
+        (g, k) for g in range(gcount) if not groups[g][2] for k in range(groups[g][1] // TILE)
+    ]
+    nz = len(owned)
     rep_id = lax.axis_index("rep")
     bal_id = lax.axis_index("bal")
     tab_id = lax.axis_index("tab")
@@ -100,24 +103,22 @@
     def y_copy(c, d, arriving=False):
         return exchange(ysend[c], yrecv[c], ys_sem, yr_sem, "bal", bal_id, nb, d, c, arriving)
 
-    def x2_copy(a, d, arriving=False):
-        return exchange(
-            xs2.at[a], xr2.at[a], xs2_sem, xr2_sem, "x", x_id, nx, d, a, arriving
-        )
-
-    def y2_copy(a, d, arriving=False):
-        return exchange(
-            ys2.at[a], yr2.at[a], ys2_sem, yr2_sem, "bal", bal_id, nb, d, a, arriving
-        )
-
-    def yb_copy(a, d, arriving=False):
-        return exchange(
-            ybs.at[a], ybr.at[a], ybs_sem, ybr_sem, "bal", bal_id, nb, d, a, arriving
-        )
-
-    def xb_copy(a, d, arriving=False):
-        return exchange(
-            xbs.at[a], xbr.at[a], xbs_sem, xbr_sem, "x", x_id, nx, d, a, arriving
+    def over(axis):
+        return ("x", x_id, nx) if axis == "x" else ("bal", bal_id, nb)
+
+    def first_copy(g, d, arriving=False):
+        axis = over(groups[g][0][0])
+        return exchange(first_out[g], first_in[g], fs_sem, fr_sem, *axis, d, g, arriving)
+
+    def next_copy(g, d, arriving=False):
+        axis = over(groups[g][0][1])
+        return exchange(next_out[g], next_in[g], ns_sem, nr_sem, *axis, d, g, arriving)
+
+    def whole_copy(k, d, arriving=False):
+        p = lax.rem(rep_id + d, nr)
+        at = p if arriving else rep_id
+        return remote(
+            whole_out[k], whole_in[k].at[at], ws_sem.at[k, p], wr_sem.at[k, at], "rep", p
         )
 
     def o_copy(x):
@@ -146,8 +147,12 @@
         for load in loads[:5]:
             load.start()
         barrier = pltpu.get_barrier_semaphore()
-        for axis, me, count in (("tab", tab_id, nt), ("bal", bal_id, nb), ("rep", rep_id, nr)):
-            for d in range(1, count):
+        for axis, me, count, reach in (
+            ("tab", tab_id, nt, range(1, nt)),
+            ("bal", bal_id, nb, range(1, nb)),
+            ("rep", rep_id, nr, (1, nr - 1)),
+        ):
+            for d in reach:
                 pl.semaphore_signal(barrier, inc=1, device_id={axis: lax.rem(me + d, count)})
         loads[0].wait()
         loads[1].wait()
@@ -167,7 +172,18 @@
                     xsend[c][2 * i + k] = block[:, firsts[c] : firsts[c] + widths[c]]
 
     def greeted():
-        pl.semaphore_wait(pltpu.get_barrier_semaphore(), nt - 1 + nb - 1 + nr - 1)
+        pl.semaphore_wait(pltpu.get_barrier_semaphore(), nt - 1 + nb - 1 + 2)
+
+    hops = nr // 2 - 1
+
+    def hop_signal(k):
+        for side in range(2):
+            peer = lax.rem(rep_id + (nr - 1 if side else 1), nr)
+            pl.semaphore_signal(hop_sem.at[k, side], inc=1, device_id={"rep": peer})
+
+    def hop_wait(k):
+        for side in range(2):
+            pl.semaphore_wait(hop_sem.at[k, side], 1)
 
     def x_start(c):
         for d in farthest_first(nt):
@@ -274,7 +290,7 @@
                 first = jnp.where(in_off[s] <= at, in_off[s], first)
             scale[i] = jnp.where((source <= at) & (source >= first), 0.5 * HEAD**-0.5, 0.0)
 
-    step = 512
+    step = 1024
     early = firsts[-1]
 
     def project_early():
@@ -298,17 +314,17 @@
         keys = slice(low, (i + 1) * TILE)
         lanes = slice(2 * TILE - (i + 1) * TILE + low, 2 * TILE)
 
-        @pl.loop(0, heads // 2)
-        def _(pair_of_heads):
-            for k in range(2):
-                def cols(part):
-                    at = part * model + (pair_of_heads * 2 + k) * HEAD
-                    return pl.ds(pl.multiple_of(at, HEAD), HEAD)
-
-                scores = dot_nt(prj[rows, cols(2)], prj[keys, cols(3)])
-                half = scores * scale[i, :, lanes]
-                weights = (half + half * jnp.tanh(half)).astype(BF16)
-                asum[rows, cols(0)] = dot_nn(weights, prj[keys, cols(1)])
+        @pl.loop(0, heads // 8)
+        def _(some):
+            def cols(part, k):
+                at = part * model + (some * 8 + k) * HEAD
+                return pl.ds(pl.multiple_of(at, HEAD), HEAD)
+
+            scores = [dot_nt(prj[rows, cols(2, k)], prj[keys, cols(3, k)]) for k in range(8)]
+            halves = [part * scale[i, :, lanes] for part in scores]
+            weights = [(half + half * jnp.tanh(half)).astype(BF16) for half in halves]
+            for k in range(8):
+                asum[rows, cols(0, k)] = dot_nn(weights[k], prj[keys, cols(1, k)])
 
     def gate(i):
         rows = slice(i * TILE, (i + 1) * TILE)
@@ -318,69 +334,56 @@
         return dot_nn(ogp[2 * x + core], att[:, cols]) + dot_nn(ogr[x], attr[:, cols])
 
     def columns(g):
-        return slice(g * gwidth, (g + 1) * gwidth)
-
-    groups = []
-    for g, kind in enumerate(gorder):
-        groups.append((kind, gorder[:g].count(kind)))
+        return slice(gfirsts[g], gfirsts[g] + groups[g][1])
 
     def grad_start(g):
-        kind, a = groups[g]
-        if kind == "A":
+        axes, width, _ = groups[g]
+        if axes == "xy":
             for d in farthest_first(nx) + [0]:
                 x = lax.rem(x_id + d, nx)
-                part = partial(x, columns(g))
+                first_out[g][x] = partial(x, columns(g)).astype(BF16)
                 if d:
-                    xs2[a, x] = part.astype(BF16)
-                    x2_copy(a, d).start()
-                else:
-                    gown[a] = part
+                    first_copy(g, d).start()
         else:
             for x in range(nx):
                 part = partial(x, columns(g)).astype(BF16)
-                ybs[a, :, x * 16 : (x + 1) * 16, :] = part.reshape(nb, 16, gwidth)
+                first_out[g][:, x * 16 : (x + 1) * 16, :] = part.reshape(nb, 16, width)
             for d in farthest_first(nb):
-                yb_copy(a, d).start()
+                first_copy(g, d).start()
+
+    def gather(axis, copy, g, own, others):
+        _, me, count = over(axis)
+        total = own[g][me].astype(F32)
+        for d in farthest_first(count)[::-1]:
+            copy(g, d, True).wait_recv()
+            total = total + others[g][lax.rem(me + d, count)].astype(F32)
+        return total.astype(BF16)
 
     def grad_turn(g):
-        kind, a = groups[g]
-        if kind == "A":
-            total = gown[a]
-            for d in farthest_first(nx):
-                x2_copy(a, d, True).wait_recv()
-                total = total + xr2[a, lax.rem(x_id + d, nx)].astype(F32)
-            ys2[a] = total.astype(BF16).reshape(nb, 16, gwidth)
-            for d in farthest_first(nb):
-                y2_copy(a, d).start()
-        else:
-            total = ybs[a, bal_id].astype(F32)
-            for d in farthest_first(nb):
-                yb_copy(a, d, True).wait_recv()
-                total = total + ybr[a, lax.rem(bal_id + d, nb)].astype(F32)
-            xbs[a] = total.astype(BF16).reshape(nx, 16, gwidth)
-            for d in farthest_first(nx):
-                xb_copy(a, d).start()
+        axes, width, _ = groups[g]
+        total = gather(axes[0], first_copy, g, first_out, first_in)
+        _, _, count = over(axes[1])
+        next_out[g][...] = total.reshape(count, 16, width)
+        for d in farthest_first(count):
+            next_copy(g, d).start()
 
     def grad_end(g):
-        kind, a = groups[g]
-        if kind == "A":
-            total = ys2[a, bal_id].astype(F32)
-            for d in farthest_first(nb):
-                y2_copy(a, d, True).wait_recv()
-                total = total + yr2[a, lax.rem(bal_id + d, nb)].astype(F32)
-        else:
-            total = xbs[a, x_id].astype(F32)
-            for d in farthest_first(nx):
-                xb_copy(a, d, True).wait_recv()
-                total = total + xbr[a, lax.rem(x_id + d, nx)].astype(F32)
-        total = total.astype(BF16)
-        for k in range(gwidth // zwidth):
-            j = g * (gwidth // zwidth) + k
-            zs[j] = total[:, k * zwidth : (k + 1) * zwidth]
-
-            @pl.when(rep_id != j)
-            def _():
-                z_copy(j).start()
+        axes, width, whole = groups[g]
+        total = gather(axes[1], next_copy, g, next_out, next_in)
+        if whole:
+            k = direct.index(g)
+            whole_out[k][...] = total
+            for d in farthest_first(nr):
+                whole_copy(k, d).start()
+            whole_in[k][rep_id] = total
+        for j in range(nz):
+            if owned[j][0] == g:
+                at = owned[j][1] * TILE
+                zs[j] = total[:, at : at + TILE]
+
+                @pl.when(rep_id != j)
+                def _():
+                    z_copy(j).start()
 
     def grad_spread():
         @pl.when(rep_id < nz)
@@ -401,7 +404,15 @@
             def _():
                 g_arrive(j).wait_recv()
 
-            grad_ref[:, j * zwidth : (j + 1) * zwidth] = zg[j]
+            at = gfirsts[owned[j][0]] + owned[j][1] * TILE
+            grad_ref[:, at : at + TILE] = zg[j]
+        for k, g in enumerate(direct):
+            for d in range(1, nr):
+                whole_copy(k, d, True).wait_recv()
+            total = whole_in[k][0].astype(F32)
+            for r in range(1, nr):
+                total = total + whole_in[k][r].astype(F32)
+            grad_ref[:, columns(g)] = total.astype(BF16)
 
     def all_sent():
         for c in range(chunks):
@@ -413,11 +424,13 @@
             o_copy(x).wait_send()
         for i in range(tiles):
             a_copy(i).wait_send()
-        for kind, a in groups:
-            for d in range(1, nx):
-                (x2_copy if kind == "A" else xb_copy)(a, d).wait_send()
-            for d in range(1, nb):
-                (y2_copy if kind == "A" else yb_copy)(a, d).wait_send()
+        for g in range(gcount):
+            for copy, axis in zip((first_copy, next_copy), groups[g][0]):
+                for d in range(1, over(axis)[2]):
+                    copy(g, d).wait_send()
+        for k in range(len(direct)):
+            for d in range(1, nr):
+                whole_copy(k, d).wait_send()
         for j in range(nz):
 
             @pl.when(rep_id != j)
@@ -432,6 +445,7 @@
     load_and_greet()
     normalize_rows()
     greeted()
+    hop_signal(0)
     for c in range(min(ahead, chunks)):
         x_start(c)
     start, length, in_off = history_bounds()
@@ -442,6 +456,10 @@
     mask_scale(in_off)
     for c in range(chunks - 1):
         y_in(c)
+        if c < hops:
+            hop_wait(c)
+            if c + 1 < hops:
+                hop_signal(c + 1)
     project_early()
     y_in(chunks - 1)
     project_late()
@@ -454,11 +472,15 @@
         o_copy(x).wait_recv()
     for i in range(tiles):
         a_copy(i).wait_recv()
-    for g in range(len(gorder)):
+    for g in range(gcount):
         grad_start(g)
-    for g in range(len(gorder)):
+    for k in range(chunks - 1, hops):
+        hop_wait(k)
+        if k + 1 < hops:
+            hop_signal(k + 1)
+    for g in range(gcount):
         grad_turn(g)
-    for g in range(len(gorder)):
+    for g in range(gcount):
         grad_end(g)
     grad_spread()
     all_sent()
@@ -471,11 +493,14 @@
     most = hot_rows.shape[0] // nt
     widths = (128, 256, 256, 256, 128)
     ahead = 2
-    gorder = "BAAA"
-    chunks, groups = len(widths), len(gorder)
-    acount, bcount = gorder.count("A"), gorder.count("B")
-    nx, gwidth, pair = nt // 2, model // groups, 2 * most
-    nz = min(nr, 8)
+    groups = (
+        ("xy", 256, False), ("yx", 256, False), ("xy", 256, True), ("yx", 128, True),
+        ("xy", 128, True),
+    )
+    chunks, gcount = len(widths), len(groups)
+    nx, pair = nt // 2, 2 * most
+    nz = sum(width // TILE for _, width, whole in groups if not whole)
+    wholes = [width for _, width, whole in groups if whole]
     vmem = pltpu.VMEM
     dma = pltpu.SemaphoreType.DMA
 
@@ -484,11 +509,22 @@
 
     x_parts = [vmem((nt, pair, width), BF16) for width in widths]
     y_parts = [vmem((nb, *y_block(width)), BF16) for width in widths]
+    def shares(axis, rows):
+        return (nx, rows // nx) if axis == "x" else (nb, rows // nb)
+
+    firsts = [vmem((*shares(axes[0], nx * nb * 16), width), BF16) for axes, width, _ in groups]
+    nexts = [vmem((nx if axes[1] == "x" else nb, 16, width), BF16) for axes, width, _ in groups]
     scratch = [
         x_parts,
         x_parts,
         y_parts,
         y_parts,
+        firsts,
+        firsts,
+        nexts,
+        nexts,
+        [vmem((16, width), BF16) for width in wholes],
+        [vmem((nr, 16, width), BF16) for width in wholes],
         vmem((1, home), jnp.int32),
         pltpu.SMEM(lengths.shape, jnp.int32),
         pltpu.SMEM(destination.shape, jnp.int32),
@@ -509,19 +545,10 @@
         vmem((home, model), F32),
         vmem((home, model), BF16),
         vmem((home, model), BF16),
-        vmem((acount, nb * 16, gwidth), F32),
-        vmem((acount, nx, nb * 16, gwidth), BF16),
-        vmem((acount, nx, nb * 16, gwidth), BF16),
-        vmem((acount, nb, 16, gwidth), BF16),
-        vmem((acount, nb, 16, gwidth), BF16),
-        vmem((bcount, nb, nx * 16, gwidth), BF16),
-        vmem((bcount, nb, nx * 16, gwidth), BF16),
-        vmem((bcount, nx, 16, gwidth), BF16),
-        vmem((bcount, nx, 16, gwidth), BF16),
-        vmem((nz, 16, model // nz), BF16),
-        vmem((nr, 16, model // nz), BF16),
-        vmem((16, model // nz), BF16),
-        vmem((nz, 16, model // nz), BF16),
+        vmem((nz, 16, TILE), BF16),
+        vmem((nr, 16, TILE), BF16),
+        vmem((16, TILE), BF16),
+        vmem((nz, 16, TILE), BF16),
         dma((8,)),
         dma((chunks, nt)),
         dma((chunks, nt)),
@@ -531,22 +558,21 @@
         dma((nx,)),
         dma((home // TILE,)),
         dma((home // TILE,)),
-        dma((acount, nx)),
-        dma((acount, nx)),
-        dma((acount, nb)),
-        dma((acount, nb)),
-        dma((bcount, nb)),
-        dma((bcount, nb)),
-        dma((bcount, nx)),
-        dma((bcount, nx)),
+        dma((gcount, max(nx, nb))),
+        dma((gcount, max(nx, nb))),
+        dma((gcount, max(nx, nb))),
+        dma((gcount, max(nx, nb))),
+        dma((len(wholes), nr)),
+        dma((len(wholes), nr)),
         dma((nz,)),
         dma((nr,)),
         dma((nr,)),
         dma((nz,)),
+        pltpu.SemaphoreType.REGULAR((nr // 2 - 1, 2)),
     ]
     hbm = pl.BlockSpec(memory_space=pl.ANY)
     return pl.pallas_call(
-        functools.partial(layer_kernel, nr, nb, nt, most, widths, ahead, gorder),
+        functools.partial(layer_kernel, nr, nb, nt, most, widths, ahead, groups),
         out_shape=(
             jax.ShapeDtypeStruct((home, model), BF16),
             jax.ShapeDtypeStruct((model // (nb * nt), model), BF16),

time: 105 us -> 100 us (0.952)
  Pallas kernels: 100 us -> 95.7 us
    pallas_call x1, Pallas kernels: 100 us -> 95.7 us  [on_device(): pl.pallas_call(functools.partial(layer_kernel, nr, nb, nt, most, widths,...]
where the time goes in v3:
time: 100 us; the launch traced here: 99.8 us
  Pallas kernels  95.7 us (96%)
  local copies, waits for them, and re-layouts  3.44 us (3%)
    pallas_call x1, Pallas kernels, on_device(): pl.pallas_call(functools.partial(layer_kernel, nr, nb, nt, most, widths,...  95.7 us
    unnamed x2, local copies, waits for them, and re-layouts  3.44 us

profile of v3, /device:TPU:1, one launch (start us, length us, event | category | flops | bytes accessed | tf_op | source)
XLA Modules:
  0.0 99.8 jit_solution(11800136684149288262)
XLA Ops:
  0.6 95.7 %shard_map.86 = (bf16[384,1024]{1,0:T(8,128)(2,1)}, bf16[16,1024]{1,0:T(8,128)(2,1)}) custom-call(f32[320,1024]{1,0:T(8,128)} %hot_hbm.1, bf16[320,1024]{1,0:T(8,128)(2,1)} %cold_hbm.1, s32[1,384]{1,0:T(1,128)} %bitcast.1, s32[1,8,1,8]{3,2,1,0:T(1,128)} %len_hbm.1, s32[1,8,1,8]{3,2,1,0:T(1,128)} %dest_hbm.1, bf16[1024,4096]{1,0:T(8,128)(2,1)} %w_hbm.1, ...), custom_call_target="tpu_custom_call" | custom-call | tf_op jit(solution)/shard_map/pallas_call | solution.py:574
  96.4 2.1 %copy.11 = bf16[384,1024]{1,0:T(8,128)(2,1)} copy(bf16[384,1024]{1,0:T(8,128)(2,1)} %get-tuple-element.4) | data formatting | bytes 1572864
  98.4 1.4 %copy.12 = bf16[16,1024]{1,0:T(8,128)(2,1)} copy(bf16[16,1024]{1,0:T(8,128)(2,1)} %get-tuple-element.5) | data formatting | bytes 65536

commit v4 on v3

--- a/solution.py
+++ b/solution.py
@@ -45,11 +45,11 @@
     nr, nb, nt, most, widths, ahead, groups,
     hot_hbm, cold_hbm, code_hbm, len_hbm, dest_hbm, w_hbm, og_hbm,
     att_hbm, grad_ref,
-    xsend, xrecv, ysend, yrecv, first_out, first_in, next_out, next_in, whole_out, whole_in,
+    xsend, xrecv, ysend, yrecv, first_out, first_in, next_out, next_in, whole_out, whole_in, gown,
     code_ref, len_ref, dest_ref,
     hot, cold, w, og, ogp, ogr, bmat, smat, spread, tmat, bal, acc, prj, scale,
     asum, att, attr, zs, zr, zo, zg,
-    load_sem, xs_sem, xr_sem, ys_sem, yr_sem, os_sem, or_sem, as_sem, ar_sem,
+    load_sem, row_sem, xs_sem, xr_sem, ys_sem, yr_sem, os_sem, or_sem, as_sem, ar_sem,
     fs_sem, fr_sem, ns_sem, nr_sem, ws_sem, wr_sem, zs_sem, zr_sem, gs_sem, gr_sem, hop_sem,
 ):
     home, model = og.shape
@@ -77,12 +77,19 @@
         pltpu.make_async_copy(src, dst, load_sem.at[i])
         for i, (src, dst) in enumerate(
             (
-                (hot_hbm, hot), (cold_hbm, cold), (code_hbm, code_ref), (len_hbm, len_ref),
-                (dest_hbm, dest_ref), (og_hbm, og), (w_hbm, w),
+                (code_hbm, code_ref), (len_hbm, len_ref), (dest_hbm, dest_ref), (og_hbm, og),
+                (w_hbm, w),
             )
         )
     ]
-    att_copy = pltpu.make_async_copy(att, att_hbm, load_sem.at[7])
+    att_copy = pltpu.make_async_copy(att, att_hbm, load_sem.at[5])
+
+    def row_loads(i):
+        rows = pl.ds(pl.multiple_of(i * 2 * most, 16), 2 * most)
+        return [
+            pltpu.make_async_copy(src.at[rows], dst.at[rows], row_sem.at[k, i])
+            for k, (src, dst) in enumerate(((hot_hbm, hot), (cold_hbm, cold)))
+        ]
 
     def remote(src, dst, send, recv, axis, peer):
         return pltpu.make_async_remote_copy(
@@ -144,7 +151,10 @@
         return remote(zo, zg.at[j], gs_sem.at[0], gr_sem.at[j], "rep", j)
 
     def load_and_greet():
-        for load in loads[:5]:
+        for i in range(nx):
+            for load in row_loads(i):
+                load.start()
+        for load in loads[:3]:
             load.start()
         barrier = pltpu.get_barrier_semaphore()
         for axis, me, count, reach in (
@@ -154,15 +164,13 @@
         ):
             for d in reach:
                 pl.semaphore_signal(barrier, inc=1, device_id={axis: lax.rem(me + d, count)})
-        loads[0].wait()
-        loads[1].wait()
-        loads[5].start()
-        loads[6].start()
 
     def normalize_rows():
         @pl.loop(0, nx)
         def _(i):
             rows = pl.ds(pl.multiple_of(i * 2 * most, 16), 2 * most)
+            for load in row_loads(i):
+                load.wait()
             hot_n = normalize(hot[rows, :])
             cold_n = normalize(cold[rows, :].astype(F32))
             for k in range(2):
@@ -172,6 +180,8 @@
                     xsend[c][2 * i + k] = block[:, firsts[c] : firsts[c] + widths[c]]
 
     def greeted():
+        for load in loads[3:]:
+            load.start()
         pl.semaphore_wait(pltpu.get_barrier_semaphore(), nt - 1 + nb - 1 + 2)
 
     hops = nr // 2 - 1
@@ -190,7 +200,7 @@
             x_copy(c, d).start()
 
     def history_bounds():
-        for load in loads[2:5]:
+        for load in loads[:3]:
             load.wait()
         start = [jnp.int32(0)] * nb
         length = [jnp.int32(0)] * nb
@@ -272,7 +282,7 @@
         bal[:, firsts[c] : firsts[c] + width] = dot_nn(tmat[...], arrived).astype(BF16)
 
     def turn_out_grad():
-        loads[5].wait()
+        loads[3].wait()
         for b in range(nb):
             cols = 16 * nt
             turned = og[:, b * cols : (b + 1) * cols].T
@@ -291,10 +301,10 @@
             scale[i] = jnp.where((source <= at) & (source >= first), 0.5 * HEAD**-0.5, 0.0)
 
     step = 1024
-    early = firsts[-1]
+    early = firsts[-2]
 
     def project_early():
-        loads[6].wait()
+        loads[4].wait()
 
         @pl.loop(0, 4 * model // step)
         def _(n):
@@ -330,8 +340,16 @@
         rows = slice(i * TILE, (i + 1) * TILE)
         att[rows, :] = (normalize(asum[rows, :]) * prj[rows, :model].astype(F32)).astype(BF16)
 
-    def partial(x, cols):
-        return dot_nn(ogp[2 * x + core], att[:, cols]) + dot_nn(ogr[x], attr[:, cols])
+    def partial_own(g):
+        for x in range(nx):
+            gown[g][x] = dot_nn(ogp[2 * x + core], att[:, columns(g)])
+
+    def partial(g, x):
+        if g < len(gown):
+            own = gown[g][x]
+        else:
+            own = dot_nn(ogp[2 * x + core], att[:, columns(g)])
+        return own + dot_nn(ogr[x], attr[:, columns(g)])
 
     def columns(g):
         return slice(gfirsts[g], gfirsts[g] + groups[g][1])
@@ -341,12 +359,12 @@
         if axes == "xy":
             for d in farthest_first(nx) + [0]:
                 x = lax.rem(x_id + d, nx)
-                first_out[g][x] = partial(x, columns(g)).astype(BF16)
+                first_out[g][x] = partial(g, x).astype(BF16)
                 if d:
                     first_copy(g, d).start()
         else:
             for x in range(nx):
-                part = partial(x, columns(g)).astype(BF16)
+                part = partial(g, x).astype(BF16)
                 first_out[g][:, x * 16 : (x + 1) * 16, :] = part.reshape(nb, 16, width)
             for d in farthest_first(nb):
                 first_copy(g, d).start()
@@ -460,7 +478,8 @@
             hop_wait(c)
             if c + 1 < hops:
                 hop_signal(c + 1)
-    project_early()
+        if c == chunks - 3:
+            project_early()
     y_in(chunks - 1)
     project_late()
     for i in range(tiles):
@@ -468,6 +487,8 @@
         gate(i)
         a_copy(i).start()
     att_copy.start()
+    for g in range(len(gown)):
+        partial_own(g)
     for x in range(nx):
         o_copy(x).wait_recv()
     for i in range(tiles):
@@ -487,6 +508,11 @@
     att_copy.wait()
 
 
+def hand_over(att_in, grad_in, att_out, grad_out):
+    att_out[...] = att_in[...]
+    grad_out[...] = grad_in[...]
+
+
 def on_device(sizes, hot_rows, cold_rows, row_source, lengths, destination, proj_weight, out_grad):
     nr, nb, nt = sizes
     home, model = out_grad.shape
@@ -525,6 +551,7 @@
         nexts,
         [vmem((16, width), BF16) for width in wholes],
         [vmem((nr, 16, width), BF16) for width in wholes],
+        [vmem((nx, nb * 16, width), F32) for _, width, _ in groups[:2]],
         vmem((1, home), jnp.int32),
         pltpu.SMEM(lengths.shape, jnp.int32),
         pltpu.SMEM(destination.shape, jnp.int32),
@@ -549,7 +576,8 @@
         vmem((nr, 16, TILE), BF16),
         vmem((16, TILE), BF16),
         vmem((nz, 16, TILE), BF16),
-        dma((8,)),
+        dma((6,)),
+        dma((2, nx)),
         dma((chunks, nt)),
         dma((chunks, nt)),
         dma((chunks, nb)),
@@ -571,7 +599,7 @@
         pltpu.SemaphoreType.REGULAR((nr // 2 - 1, 2)),
     ]
     hbm = pl.BlockSpec(memory_space=pl.ANY)
-    return pl.pallas_call(
+    att, grad = pl.pallas_call(
         functools.partial(layer_kernel, nr, nb, nt, most, widths, ahead, groups),
         out_shape=(
             jax.ShapeDtypeStruct((home, model), BF16),
@@ -592,6 +620,23 @@
         proj_weight,
         out_grad,
     )
+    parts = 3
+    return pl.pallas_call(
+        hand_over,
+        grid=(parts,),
+        out_shape=(
+            jax.ShapeDtypeStruct(att.shape, att.dtype),
+            jax.ShapeDtypeStruct(grad.shape, grad.dtype),
+        ),
+        in_specs=[
+            pl.BlockSpec((home // parts, model), lambda i: (i, 0)),
+            pl.BlockSpec(grad.shape, lambda i: (0, 0)),
+        ],
+        out_specs=(
+            pl.BlockSpec((home // parts, model), lambda i: (i, 0)),
+            pl.BlockSpec(grad.shape, lambda i: (0, 0)),
+        ),
+    )(att, grad)
 
 
 def solution(mesh):

time: 100 us -> 99.2 us (level)
  local copies, waits for them, and re-layouts: 3.44 us -> 0 us
  Pallas kernels: 95.7 us -> 98.3 us
    unnamed x2 -> x0, local copies, waits for them, and re-layouts: 3.44 us -> none
    pallas_call x0 -> x1, Pallas kernels: none -> 2.87 us  [on_device(): pl.pallas_call(hand_over, grid=(parts,), out_shape=(jax.ShapeDtypeStruct(...]
where the time goes in v4:
time: 99.2 us; the launch traced here: 99 us
  Pallas kernels  98.3 us (99%)
    pallas_call x1, Pallas kernels, on_device(): pl.pallas_call(functools.partial(layer_kernel, nr, nb, nt, most, widths,...  95.5 us
    pallas_call x1, Pallas kernels, on_device(): pl.pallas_call(hand_over, grid=(parts,), out_shape=(jax.ShapeDtypeStruct(...  2.87 us

profile of v4, /device:TPU:1, one launch (start us, length us, event | category | flops | bytes accessed | tf_op | source)
XLA Modules:
  0.0 99.0 jit_solution(213140577108529877)
XLA Ops:
  0.6 95.5 %shard_map.86 = (bf16[384,1024]{1,0:T(8,128)(2,1)}, bf16[16,1024]{1,0:T(8,128)(2,1)}) custom-call(f32[320,1024]{1,0:T(8,128)} %hot_hbm.1, bf16[320,1024]{1,0:T(8,128)(2,1)} %cold_hbm.1, s32[1,384]{1,0:T(1,128)} %bitcast.1, s32[1,8,1,8]{3,2,1,0:T(1,128)} %len_hbm.1, s32[1,8,1,8]{3,2,1,0:T(1,128)} %dest_hbm.1, bf16[1024,4096]{1,0:T(8,128)(2,1)} %w_hbm.1, ...), custom_call_target="tpu_custom_call" | custom-call | tf_op jit(solution)/shard_map/pallas_call | solution.py:602
  96.1 2.9 %shard_map.87 = (bf16[384,1024]{1,0:T(8,128)(2,1)}, bf16[16,1024]{1,0:T(8,128)(2,1)}) custom-call(bf16[384,1024]{1,0:T(8,128)(2,1)} %get-tuple-element.4.att_in, bf16[16,1024]{1,0:T(8,128)(2,1)} %get-tuple-element.5.grad_in), custom_call_target="tpu_custom_call" | custom-call | tf_op jit(solution)/shard_map/pallas_call | solution.py:624

commit v5 on v4

--- a/solution.py
+++ b/solution.py
@@ -508,9 +508,22 @@
     att_copy.wait()
 
 
-def hand_over(att_in, grad_in, att_out, grad_out):
-    att_out[...] = att_in[...]
-    grad_out[...] = grad_in[...]
+def hand_over(parts, att_in, grad_in, att_out, grad_out, att, grad, in_sem, out_sem):
+    rows = att.shape[0] // parts
+    views = [pl.ds(i * rows, rows) for i in range(parts)]
+    steps = [(grad_in, grad, grad_out)]
+    steps += [(att_in.at[view], att.at[view], att_out.at[view]) for view in views]
+    fetches, stores = [], []
+    for i, (source, held, target) in enumerate(steps):
+        fetches.append(pltpu.make_async_copy(source, held, in_sem.at[i]))
+        stores.append(pltpu.make_async_copy(held, target, out_sem.at[i]))
+    for fetch in fetches:
+        fetch.start()
+    for fetch, store in zip(fetches, stores):
+        fetch.wait()
+        store.start()
+    for store in stores:
+        store.wait()
 
 
 def on_device(sizes, hot_rows, cold_rows, row_source, lengths, destination, proj_weight, out_grad):
@@ -620,22 +633,21 @@
         proj_weight,
         out_grad,
     )
-    parts = 3
+    parts = 4
     return pl.pallas_call(
-        hand_over,
-        grid=(parts,),
+        functools.partial(hand_over, parts),
         out_shape=(
             jax.ShapeDtypeStruct(att.shape, att.dtype),
             jax.ShapeDtypeStruct(grad.shape, grad.dtype),
         ),
-        in_specs=[
-            pl.BlockSpec((home // parts, model), lambda i: (i, 0)),
-            pl.BlockSpec(grad.shape, lambda i: (0, 0)),
+        in_specs=[hbm, hbm],
+        out_specs=(hbm, hbm),
+        scratch_shapes=[
+            vmem(att.shape, att.dtype),
+            vmem(grad.shape, grad.dtype),
+            dma((parts + 1,)),
+            dma((parts + 1,)),
         ],
-        out_specs=(
-            pl.BlockSpec((home // parts, model), lambda i: (i, 0)),
-            pl.BlockSpec(grad.shape, lambda i: (0, 0)),
-        ),
     )(att, grad)
 
 

time: 99.2 us -> 98.3 us (level)
  no operation moved by 1% of the time
where the time goes in v5:
time: 98.3 us; the launch traced here: 98.1 us
  Pallas kernels  97.5 us (99%)
    pallas_call x1, Pallas kernels, on_device(): pl.pallas_call(functools.partial(layer_kernel, nr, nb, nt, most, widths,...  95.5 us
    pallas_call x1, Pallas kernels, on_device(): pl.pallas_call(functools.partial(hand_over, parts), out_shape=(jax.ShapeD...  2 us

profile of v5, /device:TPU:1, one launch (start us, length us, event | category | flops | bytes accessed | tf_op | source)
XLA Modules:
  0.0 98.1 jit_solution(4604079500231144453)
XLA Ops:
  0.6 95.5 %shard_map.86 = (bf16[384,1024]{1,0:T(8,128)(2,1)}, bf16[16,1024]{1,0:T(8,128)(2,1)}) custom-call(f32[320,1024]{1,0:T(8,128)} %hot_hbm.1, bf16[320,1024]{1,0:T(8,128)(2,1)} %cold_hbm.1, s32[1,384]{1,0:T(1,128)} %bitcast.1, s32[1,8,1,8]{3,2,1,0:T(1,128)} %len_hbm.1, s32[1,8,1,8]{3,2,1,0:T(1,128)} %dest_hbm.1, bf16[1024,4096]{1,0:T(8,128)(2,1)} %w_hbm.1, ...), custom_call_target="tpu_custom_call" | custom-call | tf_op jit(solution)/shard_map/pallas_call | solution.py:615
  96.1 2.0 %shard_map.87 = (bf16[384,1024]{1,0:T(8,128)(2,1)}, bf16[16,1024]{1,0:T(8,128)(2,1)}) custom-call(bf16[384,1024]{1,0:T(8,128)(2,1)} %get-tuple-element.4.att_in, bf16[16,1024]{1,0:T(8,128)(2,1)} %get-tuple-element.5.grad_in), custom_call_target="tpu_custom_call" | custom-call | tf_op jit(solution)/shard_map/pallas_call | solution.py:637
